TPU v7x, 512 devices: a whole 4x8x8 slice. The times are simulated.
512 devices in a mesh: dp: 4 (over z_hi, core), expert: 16 (over z_lo, x), tensor: 8 (over y).
Axes of the slice: x: 4, y: 8, z: 8 (z_hi: 2, z_lo: 4; z = z_hi * 4 + z_lo), core: 2. Of those that a mesh axis runs over, the one named last changes fastest.
Arguments:
- x_rows: bfloat16 [1536, 3072], P(('dp', 'expert'), 'tensor'), may hold values from -6 to 6
- cotangent: bfloat16 [1536, 3072], P(('dp', 'expert'), 'tensor'), may hold values from -6 to 6
- expert_ids: int32 [1536, 4], P(('dp', 'expert')), may hold values from 0 to 15, all different within a row; in each aligned block of 24 rows (0 to 23, 24 to 47, ...) at most 8 rows name the same one
- route_weight: float32 [1536, 4], P(('dp', 'expert')), may hold values from 0.1 to 1
- gate_weight: bfloat16 [16, 3072, 5376], P('expert', 'dp', 'tensor'), may hold values from -0.109375 to 0.109375
- up_weight: bfloat16 [16, 3072, 5376], P('expert', 'dp', 'tensor'), may hold values from -0.109375 to 0.109375
- down_weight: bfloat16 [16, 5376, 3072], P('expert', 'tensor', 'dp'), may hold values from -0.078125 to 0.078125
Outputs:
- input_grad: bfloat16 [1536, 3072], P(('dp', 'expert'), 'tensor')
- down_grad: bfloat16 [16, 5376, 3072], P('expert', 'tensor', 'dp')
Inputs may be any that keep to these rules, and one draw needn't show every extreme that they name: `expert_ids`: each token names 4 different experts. In each aligned block of 24 rows (the tokens of one index of dp and expert) no expert is named by more than 8 rows, a bound that some block reaches.
All inputs are finite; a program needn't handle non-finite values.
Results may differ from a plain program's by a relative error of at most 0.0064.
Values may be sent and summed in bfloat16 or wider, within the bound.
No kernel may reach another device: no remote copies, remote signals or barrier semaphores. Data moves between devices by JAX's collectives and lax.ppermute only.
A program may use at most 64 MiB of HBM per device.

v0:
```python
import jax
import jax.numpy as jnp
from jax import lax
from jax.sharding import PartitionSpec as P

CAP = 8


def route_tables(expert_ids, route_weight, experts, capacity):
    onehot = (expert_ids[:, :, None] == jnp.arange(experts, dtype=jnp.int32)[None, None, :]).astype(
        jnp.int32
    )
    per_token = jnp.sum(onehot, axis=1)
    before = jnp.cumsum(per_token, axis=0) - per_token
    slot = jnp.sum(onehot * before[:, None, :], axis=2)
    target = expert_ids * capacity + slot
    places = jnp.arange(experts * capacity, dtype=jnp.int32)
    match = (target[:, :, None] == places[None, None, :]).astype(jnp.float32)
    select = jnp.sum(match, axis=1).astype(jnp.bfloat16)
    slot_weight = jnp.sum(match * route_weight[:, :, None], axis=(0, 1))
    return (select, slot_weight)


def per_device(x_rows, cotangent, expert_ids, route_weight, gate_weight, up_weight, down_weight):
    groups = lax.axis_size("expert")
    local = gate_weight.shape[0]
    experts = local * groups
    whole_x, whole_dy = (
        lax.all_gather(x_rows, "tensor", axis=1, tiled=True),
        lax.all_gather(cotangent, "tensor", axis=1, tiled=True),
    )
    width = whole_x.shape[1]
    select, slot_weight = route_tables(expert_ids, route_weight, experts, CAP)
    contract_rows = (((0,), (0,)), ((), ()))
    send_x = lax.dot_general(
        select, whole_x, contract_rows, preferred_element_type=jnp.float32
    ).astype(jnp.bfloat16)
    send_dy = lax.dot_general(select, whole_dy, contract_rows, preferred_element_type=jnp.float32)
    send_dy = (send_dy * slot_weight[:, None]).astype(jnp.bfloat16)
    got_x, got_dy = (
        lax.all_to_all(send_x, "expert", split_axis=0, concat_axis=0, tiled=True),
        lax.all_to_all(send_dy, "expert", split_axis=0, concat_axis=0, tiled=True),
    )
    got_x = got_x.reshape(groups, local, CAP, width)
    got_dy = got_dy.reshape(groups, local, CAP, width)
    full_gate, full_up = (
        lax.all_gather(gate_weight, "dp", axis=1, tiled=True),
        lax.all_gather(up_weight, "dp", axis=1, tiled=True),
    )
    gate = jnp.einsum("nlsd,ldf->nlsf", got_x, full_gate, preferred_element_type=jnp.float32)
    up = jnp.einsum("nlsd,ldf->nlsf", got_x, full_up, preferred_element_type=jnp.float32)
    sigma = jax.nn.sigmoid(gate)
    active = gate * sigma
    hidden = (active * up).astype(jnp.bfloat16)
    quarters = lax.all_to_all(got_dy, "dp", split_axis=3, concat_axis=0, tiled=True)
    every_hidden = lax.all_gather(hidden, "dp", axis=0, tiled=True)
    full_down = lax.all_gather(down_weight, "dp", axis=2, tiled=True)
    hidden_grad = jnp.einsum(
        "nlsd,lfd->nlsf", got_dy, full_down, preferred_element_type=jnp.float32
    )
    down_grad = jnp.einsum(
        "nlsf,nlsd->lfd", every_hidden, quarters, preferred_element_type=jnp.float32
    )
    down_grad = down_grad.astype(jnp.bfloat16)
    gate_grad = (hidden_grad * up * sigma * (1.0 + gate * (1.0 - sigma))).astype(jnp.bfloat16)
    up_grad = (hidden_grad * active).astype(jnp.bfloat16)
    slot_count = groups * local * CAP
    term = jnp.einsum("nlsf,lcf->cnls", gate_grad, full_gate, preferred_element_type=jnp.float32)
    term = term + jnp.einsum("nlsf,lcf->cnls", up_grad, full_up, preferred_element_type=jnp.float32)
    row_grad = lax.psum_scatter(
        term.reshape(x_rows.shape[1] * lax.axis_size("tensor"), slot_count),
        "tensor",
        scatter_dimension=0,
        tiled=True,
    ).astype(jnp.bfloat16)
    returned = lax.all_to_all(row_grad, "expert", split_axis=1, concat_axis=1, tiled=True)
    input_grad = lax.dot_general(
        select, returned, (((1,), (1,)), ((), ())), preferred_element_type=jnp.float32
    )
    return (input_grad.astype(jnp.bfloat16), down_grad)


def solution(mesh):
    placed = (
        P(("dp", "expert"), "tensor"),
        P(("dp", "expert"), "tensor"),
        P(("dp", "expert"), None),
        P(("dp", "expert"), None),
        P("expert", "dp", "tensor"),
        P("expert", "dp", "tensor"),
        P("expert", "tensor", "dp"),
    )
    return jax.shard_map(
        per_device,
        mesh=mesh,
        in_specs=placed,
        out_specs=(P(("dp", "expert"), "tensor"), P("expert", "tensor", "dp")),
        check_vma=False,
    )
```

profile of v0, /device:TPU:1, one launch (start us, length us, event | category | flops | bytes accessed | tf_op | source)
XLA Modules:
  0.0 329.7 jit_solution(2087817391866273682)
XLA Ops:
  7.2 0.7 all-gather.8.cloned.1.call-update
  8.0 0.7 all-gather.6.cloned.1.call-update
  9.4 0.7 convert_reduce_fusion.1
  10.3 20.9 %all_gather.20 = bf16[24,3072]{1,0:T(8,128)(2,1)S(1)} all-gather(bf16[24,384]{1,0:T(8,128)(2,1)} %param.7), channel_id=1, replica_groups=mesh['dp'=4,'expert'=16,'tensor'=8] {'tensor'}, dimensions={1}, use_global_device_ids=true | all-gather | bytes 165888 | tf_op jit(solution)/shard_map/all_gather | solution.py:29
  31.2 0.7 select_reduce_fusion.1
  31.9 0.7 multiply_add_fusion
  32.6 0.8 select_reduce_fusion
  33.4 1.3 fusion.17
  34.6 9.9 %all-to-all-start.1 = ((bf16[16,8,3072]{2,1,0:T(8,128)(2,1)}), bf16[16,8,3072]{2,1,0:T(8,128)(2,1)S(1)}, u32[]{:S(2)}, u32[]{:S(2)}) async-start(bf16[16,8,3072]{2,1,0:T(8,128)(2,1)} %fusion.17), calls=%async_computation.1 | async-start | bytes 1572864 | tf_op jit(solution)/shard_map/all_to_all | solution.py:41
  44.6 21.1 %all_gather.18 = bf16[24,3072]{1,0:T(8,128)(2,1)S(1)} all-gather(bf16[24,384]{1,0:T(8,128)(2,1)S(1)} %copy-done.2), channel_id=1, replica_groups=mesh['dp'=4,'expert'=16,'tensor'=8] {'tensor'}, dimensions={1}, use_global_device_ids=true | all-gather | bytes 165888 | tf_op jit(solution)/shard_map/all_gather | solution.py:30
  65.7 1.3 fusion.18
  67.0 29.5 %all-to-all-done.1 = bf16[16,8,3072]{2,1,0:T(8,128)(2,1)S(1)} async-done(((bf16[16,8,3072]{2,1,0:T(8,128)(2,1)}), bf16[16,8,3072]{2,1,0:T(8,128)(2,1)S(1)}, u32[]{:S(2)}, u32[]{:S(2)}) %all-to-all-start.1) | async-done | bytes 786464 | tf_op jit(solution)/shard_map/all_to_all | solution.py:41
  96.6 5.7 %all-to-all-start = ((bf16[16,8,3072]{2,1,0:T(8,128)(2,1)}), bf16[16,8,3072]{2,1,0:T(8,128)(2,1)S(1)}, u32[]{:S(2)}, u32[]{:S(2)}) async-start(bf16[16,8,3072]{2,1,0:T(8,128)(2,1)} %fusion.18), calls=%async_computation | async-start | bytes 1572864 | tf_op jit(solution)/shard_map/all_to_all | solution.py:42
  102.4 3.5 %fusion.26 = f32[16,1,8,672]{3,2,0,1:T(8,128)S(1)} fusion(bf16[16,8,3072]{2,1,0:T(8,128)(2,1)S(1)} %all-to-all-done.1, bf16[1,3072,672]{1,2,0:T(8,128)(2,1)} %all-gather.8.cloned.1.call-done), kind=kOutput, calls=%fused_computation.21 | convolution fusion | flops 528482304 | bytes 5259264 | tf_op jit(solution)/shard_map/nlsd,ldf->nlsf/dot_general | solution.py:50
  105.9 59.8 %all-gather.6.cloned.1.call-done = bf16[1,3072,672]{1,2,0:T(8,128)(2,1)} async-done(((bf16[1,768,672]{1,2,0:T(8,128)(2,1)}), bf16[1,3072,672]{1,2,0:T(8,128)(2,1)}) %all-gather.6.cloned.1.call-update) | async-done | bytes 4128784 | tf_op jit(solution)/shard_map/all_gather | solution.py:48
  165.7 3.5 %fusion.23 = f32[16,1,8,672]{3,2,0,1:T(8,128)S(1)} fusion(bf16[16,8,3072]{2,1,0:T(8,128)(2,1)S(1)} %all-to-all-done.1, bf16[1,3072,672]{1,2,0:T(8,128)(2,1)} %all-gather.6.cloned.1.call-done), kind=kOutput, calls=%fused_computation.20 | convolution fusion | flops 528482304 | bytes 5259264 | tf_op jit(solution)/shard_map/nlsd,ldf->nlsf/dot_general | solution.py:51
  169.3 66.3 %all-gather.4.cloned.1.call-done = bf16[1,672,3072]{2,1,0:T(8,128)(2,1)} async-done(((bf16[1,672,768]{2,1,0:T(8,128)(2,1)}), bf16[1,672,3072]{2,1,0:T(8,128)(2,1)}) %all-gather.4.cloned.1.call-update) | async-done | bytes 4128784 | tf_op jit(solution)/shard_map/all_gather | solution.py:57
  235.6 3.7 %fusion.20 = f32[16,1,8,672]{3,2,0,1:T(8,128)S(1)} fusion(bf16[16,8,3072]{2,1,0:T(8,128)(2,1)S(1)} %all-to-all-done, bf16[1,672,3072]{2,1,0:T(8,128)(2,1)} %all-gather.4.cloned.1.call-done), kind=kOutput, calls=%fused_computation.19 | convolution fusion | flops 528482304 | bytes 5259264 | tf_op jit(solution)/shard_map/nlsd,lfd->nlsf/dot_general | solution.py:58
  239.3 0.9 fusion
  240.2 1.3 copy-done.1
  241.5 2.0 fusion.13
  243.5 5.7 %copy.33 = bf16[16,1,8,3072]{0,2,1,3:T(8,128)(2,1)} copy(bf16[16,1,8,3072]{3,2,0,1:T(8,128)(2,1)S(1)} %bitcast.92) | data formatting | bytes 1572864 | tf_op jit(solution)/shard_map/reshape | solution.py:45
  249.2 7.8 %reshape.86 = bf16[4,2,49152]{2,1,0:T(2,128)(2,1)S(1)} reshape(bf16[3072,1,8,16]{3,2,1,0:T(8,128)(2,1)} %bitcast.90) | data formatting | bytes 1572864
  257.0 21.5 %all_to_all.45 = bf16[4,2,49152]{2,1,0:T(2,128)(2,1)S(1)} all-to-all(bf16[4,2,49152]{2,1,0:T(2,128)(2,1)S(1)} %reshape.86), channel_id=1, replica_groups=mesh['dp'=4,'expert'=16,'tensor'=8] {'dp'}, dimensions={0} | all-to-all | bytes 1572864 | tf_op jit(solution)/shard_map/all_to_all | solution.py:55
  278.5 5.6 %reshape.87 = bf16[3072,1,8,16]{3,2,1,0:T(8,128)(2,1)} reshape(bf16[4,2,49152]{2,1,0:T(2,128)(2,1)S(1)} %all_to_all.45) | data formatting | bytes 1572864
  284.2 6.3 %copy.34 = bf16[16,1,8,4,768]{4,0,3,2,1:T(8,128)(2,1)S(1)} copy(bf16[16,1,8,4,768]{0,2,4,3,1:T(8,128)(2,1)} %bitcast.91) | data formatting | bytes 1572864 | tf_op jit(solution)/shard_map/all_to_all | solution.py:55
  290.6 13.2 %all_gather.23 = bf16[64,1,8,672]{3,2,1,0:T(8,128)(2,1)S(1)} all-gather(bf16[16,1,8,672]{3,2,1,0:T(8,128)(2,1)S(1)} %fusion.34), channel_id=1, replica_groups=mesh['dp'=4,'expert'=16,'tensor'=8] {'dp'}, dimensions={0}, use_global_device_ids=true | all-gather | bytes 860160 | tf_op jit(solution)/shard_map/all_gather | solution.py:56
  303.8 1.6 convert_bitcast_fusion
  305.4 9.5 %all-to-all-start.2 = ((bf16[384,16,8]{0,2,1:T(8,128)(2,1)}), bf16[384,16,8]{0,2,1:T(8,128)(2,1)S(1)}, u32[]{:S(2)}, u32[]{:S(2)}) async-start(bf16[384,16,8]{0,2,1:T(8,128)(2,1)} %convert_bitcast_fusion), calls=%async_computation.3 | async-start | bytes 196608 | tf_op jit(solution)/shard_map/all_to_all | solution.py:76
  314.9 1.7 fusion.19
  316.6 5.8 %all-to-all-done.2 = bf16[384,16,8]{0,2,1:T(8,128)(2,1)S(1)} async-done(((bf16[384,16,8]{0,2,1:T(8,128)(2,1)}), bf16[384,16,8]{0,2,1:T(8,128)(2,1)S(1)}, u32[]{:S(2)}, u32[]{:S(2)}) %all-to-all-start.2) | async-done | bytes 98336 | tf_op jit(solution)/shard_map/all_to_all | solution.py:76
  322.4 0.7 convolution_convert_fusion.1
  (19 shorter events, 1.2 us)
Async XLA Ops:
  7.2 37.4 %copy-start.2 = (bf16[24,384]{1,0:T(8,128)(2,1)S(1)}, bf16[24,384]{1,0:T(8,128)(2,1)}, u32[]{:S(2)}) copy-start(bf16[24,384]{1,0:T(8,128)(2,1)} %param.8) | copy-start | bytes 55300
  7.2 95.2 %all-gather.8.cloned.1.call-start = ((), (), s32[]{:S(2)}) async-start(), calls=%async_computation.7 | async-start | bytes 5160960 | tf_op jit(solution)/shard_map/all_gather | solution.py:47
  7.9 157.8 %all-gather.6.cloned.1.call-start = ((), (), s32[]{:S(2)}) async-start(), calls=%async_computation.6 | async-start | bytes 5160960 | tf_op jit(solution)/shard_map/all_gather | solution.py:48
  8.7 227.0 %all-gather.4.cloned.1.call-start = ((), (), s32[]{:S(2)}) async-start(), calls=%async_computation.5 | async-start | bytes 5160960 | tf_op jit(solution)/shard_map/all_gather | solution.py:57
  34.6 61.9 %all-to-all-start.1 = ((bf16[16,8,3072]{2,1,0:T(8,128)(2,1)}), bf16[16,8,3072]{2,1,0:T(8,128)(2,1)S(1)}, u32[]{:S(2)}, u32[]{:S(2)}) async-start(bf16[16,8,3072]{2,1,0:T(8,128)(2,1)} %fusion.17), calls=%async_computation.1 | async-start | bytes 1572864 | tf_op jit(solution)/shard_map/all_to_all | solution.py:41
  96.6 72.7 %all-to-all-start = ((bf16[16,8,3072]{2,1,0:T(8,128)(2,1)}), bf16[16,8,3072]{2,1,0:T(8,128)(2,1)S(1)}, u32[]{:S(2)}, u32[]{:S(2)}) async-start(bf16[16,8,3072]{2,1,0:T(8,128)(2,1)} %fusion.18), calls=%async_computation | async-start | bytes 1572864 | tf_op jit(solution)/shard_map/all_to_all | solution.py:42
  102.3 201.5 %reduce-scatter.2.cloned.1.call-start = ((), (), s32[]{:S(2)}) async-start(), calls=%async_computation.8 | async-start | bytes 1769472 | tf_op jit(solution)/shard_map/reduce_scatter | solution.py:70
  235.6 3.7 %copy-start = (bf16[1,3072,672]{1,2,0:T(8,128)(2,1)S(1)}, bf16[1,3072,672]{1,2,0:T(8,128)(2,1)}, u32[]{:S(2)}) copy-start(bf16[1,3072,672]{1,2,0:T(8,128)(2,1)} %all-gather.8.cloned.1.call-done) | copy-start | bytes 12386308
  239.3 2.2 copy-start.1
  305.4 17.0 %all-to-all-start.2 = ((bf16[384,16,8]{0,2,1:T(8,128)(2,1)}), bf16[384,16,8]{0,2,1:T(8,128)(2,1)S(1)}, u32[]{:S(2)}, u32[]{:S(2)}) async-start(bf16[384,16,8]{0,2,1:T(8,128)(2,1)} %convert_bitcast_fusion), calls=%async_computation.3 | async-start | bytes 196608 | tf_op jit(solution)/shard_map/all_to_all | solution.py:76
Sparse Core Ops, SparseCore 0:
  10.1 85.6 all-gather.7
  97.9 67.7 all-gather.5
  167.8 67.7 all-gather.3
  243.6 34.9 reduce-scatter.1
where the time goes:
time: 331 us; the launch traced here: 330 us
  waiting for transfers between devices  164 us (50%)
  blocking collectives  76.7 us (23%)
  local copies, waits for them, and re-layouts  26.8 us (8%)
  starting transfers between devices  25.3 us (8%)
  matrix products  18.7 us (6%)
  between operations  13.9 us (4%)
  other arithmetic  4.63 us (1%)
    all_gather x1, waiting for transfers between devices, per_device(): full_down = lax.all_gather(down_weight, 'dp', axis=2, tiled=True)  66.3 us
    all_gather x1, waiting for transfers between devices, per_device(): lax.all_gather(up_weight, 'dp', axis=1, tiled=True)  59.8 us
    all_to_all x1, waiting for transfers between devices, per_device(): lax.all_to_all(send_x, 'expert', split_axis=0, concat_axis=0, tiled=True)  29.5 us
    all_to_all x1, blocking collectives, per_device(): lax.all_to_all(got_dy, 'dp', split_axis=3, concat_axis=0, tiled=True)  21.5 us
    all_gather x1, blocking collectives, per_device(): lax.all_gather(cotangent, 'tensor', axis=1, tiled=True)  21.1 us
    all_gather x1, blocking collectives, per_device(): lax.all_gather(x_rows, 'tensor', axis=1, tiled=True)  20.9 us
    unnamed x8, local copies, waits for them, and re-layouts  14.7 us
    all_gather x1, blocking collectives, per_device(): every_hidden = lax.all_gather(hidden, 'dp', axis=0, tiled=True)  13.2 us
  transfers between devices with their start and end apart: 7, of which 4 were waited for; matrix products, arithmetic and copies ran while one was open for 12% of the time, Pallas kernels for 0%

commit v1 on v0

v1 whole, which is shorter than its diff:
```python
import jax
import jax.numpy as jnp
from jax import lax
from jax.sharding import Mesh, PartitionSpec as P

CAP = 8
BF16 = jnp.bfloat16
F32 = jnp.float32
AXES = ("z_hi", "core", "z_lo", "x", "tensor")
BLOCKS = ("z_hi", "core", "z_lo", "x")
EXPERT = ("z_lo", "x")
SIDES = ("z_hi", "z_lo", "x")
SWAP = [(0, 1), (1, 0)]


def route_tables(expert_ids, route_weight, experts, capacity):
    onehot = (expert_ids[:, :, None] == jnp.arange(experts, dtype=jnp.int32)[None, None, :]).astype(
        jnp.int32
    )
    per_token = jnp.sum(onehot, axis=1)
    before = jnp.cumsum(per_token, axis=0) - per_token
    slot = jnp.sum(onehot * before[:, None, :], axis=2)
    target = expert_ids * capacity + slot
    places = jnp.arange(experts * capacity, dtype=jnp.int32)
    match = (target[:, :, None] == places[None, None, :]).astype(F32)
    select = jnp.sum(match, axis=1).astype(BF16)
    slot_weight = jnp.sum(match * route_weight[:, :, None], axis=(0, 1))
    return (select, slot_weight)


def dot(a, b, ca, cb):
    return lax.dot_general(a, b, (((ca,), (cb,)), ((), ())), preferred_element_type=F32)


def order_quarters(value, axis):
    shape = value.shape
    halves = value.reshape(shape[:axis] + (2, 2, shape[axis] // 4) + shape[axis + 1 :])
    flipped = jnp.flip(halves, axis=axis + 1)
    return jnp.where(lax.axis_index("core") == 0, halves, flipped).reshape(shape)


def per_device(x_rows, cotangent, expert_ids, route_weight, gate_weight, up_weight, down_weight):
    tensor = lax.axis_size("tensor")
    experts = lax.axis_size(EXPERT)
    tokens, piece = x_rows.shape
    own_gate, own_up, own_down = gate_weight[0], up_weight[0], down_weight[0]
    far_gate, far_up, far_down = (
        lax.ppermute(own_gate, "core", SWAP),
        lax.ppermute(own_up, "core", SWAP),
        lax.ppermute(own_down, "core", SWAP),
    )
    quarter = own_gate.shape[0]
    hidden_units = own_gate.shape[1]

    both = jnp.concatenate([x_rows, cotangent], axis=0)
    both = lax.all_to_all(
        jnp.broadcast_to(both[None], (tensor,) + both.shape), "tensor", 0, 0, tiled=True
    )
    both = order_quarters(both, 0)
    both = jnp.transpose(both, (1, 0, 2)).reshape(2 * tokens, tensor * piece)
    select, slot_weight = route_tables(expert_ids, route_weight, experts, CAP)
    places = experts * CAP

    def dispatch(rows, scale):
        halves = [
            dot(select, rows[:, z * 2 * quarter : (z + 1) * 2 * quarter], 0, 0) for z in range(2)
        ]
        if scale is not None:
            halves = [half * scale[:, None] for half in halves]
        sent = jnp.concatenate([half.astype(BF16) for half in halves], axis=0)
        got = lax.all_to_all(
            sent.reshape(2 * experts, CAP, 2 * quarter), SIDES, 0, 0, tiled=True
        )
        return got.reshape(2 * places, 2 * quarter)

    got_x = dispatch(both[:tokens], None)
    gate = dot(own_gate, got_x[:, :quarter], 0, 1) + dot(far_gate, got_x[:, quarter:], 0, 1)
    up = dot(own_up, got_x[:, :quarter], 0, 1) + dot(far_up, got_x[:, quarter:], 0, 1)
    crossed = lax.ppermute(
        jnp.concatenate([gate.astype(BF16), up.astype(BF16)], axis=0), "z_hi", SWAP
    )
    got_dy = dispatch(both[tokens:], slot_weight)
    swapped_dy = lax.ppermute(got_dy[:, quarter:], "core", SWAP)
    hidden_grad = dot(own_down, got_dy[:, :quarter], 1, 1) + dot(
        far_down, got_dy[:, quarter:], 1, 1
    )
    crossed_grad = lax.ppermute(hidden_grad.astype(BF16), "z_hi", SWAP)

    gate = gate + crossed[:hidden_units].astype(F32)
    up = up + crossed[hidden_units:].astype(F32)
    sigma = jax.nn.sigmoid(gate)
    active = gate * sigma
    hidden = (active * up).astype(BF16)
    swapped_hidden = lax.ppermute(hidden, "core", SWAP)
    slope = up * sigma * (1.0 + gate * (1.0 - sigma))
    hidden_grad = hidden_grad + crossed_grad.astype(F32)
    gate_grad = (hidden_grad * slope).astype(BF16)
    up_grad = (hidden_grad * active).astype(BF16)

    own_term = dot(gate_grad, own_gate, 0, 1) + dot(up_grad, own_up, 0, 1)
    far_term = dot(gate_grad, far_gate, 0, 1) + dot(up_grad, far_up, 0, 1)
    term = jnp.concatenate([own_term.astype(BF16), far_term.astype(BF16)], axis=1)
    returned = lax.all_to_all(
        term.reshape(2 * experts, CAP, 2 * quarter), SIDES, 0, 0, tiled=True
    ).reshape(2, places, 2 * quarter)
    mixed = jnp.concatenate([dot(select, returned[z], 1, 0) for z in range(2)], axis=1)
    mixed = jnp.transpose(mixed.astype(BF16).reshape(tokens, tensor, piece), (1, 0, 2))
    mixed = lax.all_to_all(order_quarters(mixed, 0), "tensor", 0, 0, tiled=True)
    input_grad = jnp.sum(mixed.astype(F32), axis=0).astype(BF16)

    down_grad = dot(hidden, got_dy[:, :quarter], 1, 0) + dot(swapped_hidden, swapped_dy, 1, 0)
    return (input_grad, down_grad.astype(BF16)[None])


def solution(mesh):
    fine = Mesh(mesh.devices.reshape(2, 2, 4, 4, 8), AXES)
    placed = (
        P(BLOCKS, "tensor"),
        P(BLOCKS, "tensor"),
        P(BLOCKS, None),
        P(BLOCKS, None),
        P(EXPERT, ("z_hi", "core"), "tensor"),
        P(EXPERT, ("z_hi", "core"), "tensor"),
        P(EXPERT, "tensor", ("z_hi", "core")),
    )
    return jax.shard_map(
        per_device,
        mesh=fine,
        in_specs=placed,
        out_specs=(P(BLOCKS, "tensor"), P(EXPERT, "tensor", ("z_hi", "core"))),
        check_vma=False,
    )
```

time: 331 us -> 186 us (0.56)
  the two profiles are of different devices: /device:TPU:1 before, /device:TPU:2 now
where the time goes in v1:
time: 186 us; the launch traced here: 185 us
  starting transfers between devices  91.5 us (49%)
  waiting for transfers between devices  61.6 us (33%)
  matrix products  17.8 us (10%)
  other arithmetic  11.1 us (6%)
    ppermute x1, starting transfers between devices, per_device(): crossed_grad = lax.ppermute(hidden_grad.astype(BF16), 'z_hi', SWAP)  28.3 us
    all_to_all x2, waiting for transfers between devices, dispatch(): lax.all_to_all(sent.reshape(2 * experts, CAP, 2 * quarter), SIDES, 0, 0,...  24.3 us
    all_to_all x2, starting transfers between devices, dispatch(): lax.all_to_all(sent.reshape(2 * experts, CAP, 2 * quarter), SIDES, 0, 0,...  19 us
    dot_general x18, matrix products, dot(): lax.dot_general(a, b, (((ca,), (cb,)), ((), ())), preferred_element_type=...  17.8 us
    all_to_all x1, waiting for transfers between devices, per_device(): lax.all_to_all(term.reshape(2 * experts, CAP, 2 * quarter), SIDES, 0, 0,...  13.4 us
    all_to_all x1, starting transfers between devices, per_device(): lax.all_to_all(term.reshape(2 * experts, CAP, 2 * quarter), SIDES, 0, 0,...  11.4 us
    all_to_all x1, waiting for transfers between devices, per_device(): lax.all_to_all(jnp.broadcast_to(both[None], (tensor,) + both.shape), 'ten...  9.51 us
    ppermute x1, waiting for transfers between devices, per_device(): crossed_grad = lax.ppermute(hidden_grad.astype(BF16), 'z_hi', SWAP)  7.97 us
  transfers between devices with their start and end apart: 12, of which 6 were waited for; matrix products, arithmetic and copies ran while one was open for 10% of the time, Pallas kernels for 0%

profile of v1, /device:TPU:2, one launch (start us, length us, event | category | flops | bytes accessed | tf_op | source)
XLA Modules:
  0.0 184.6 jit_solution(6855992789738737679)
XLA Ops:
  2.1 7.1 %all-to-all-start = ((bf16[8,48,384]{2,1,0:T(8,128)(2,1)}), bf16[8,48,384]{2,1,0:T(8,128)(2,1)S(1)}, u32[]{:S(2)}, u32[]{:S(2)}) async-start(bf16[8,48,384]{2,1,0:T(8,128)(2,1)} %broadcast_in_dim.4), calls=%async_computation | async-start | bytes 589824 | tf_op jit(solution)/shard_map/all_to_all | solution.py:56
  11.5 0.8 select_reduce_fusion
  12.3 9.5 %all-to-all-done = bf16[8,48,384]{2,1,0:T(8,128)(2,1)S(1)} async-done(((bf16[8,48,384]{2,1,0:T(8,128)(2,1)}), bf16[8,48,384]{2,1,0:T(8,128)(2,1)S(1)}, u32[]{:S(2)}, u32[]{:S(2)}) %all-to-all-start) | async-done | bytes 294944 | tf_op jit(solution)/shard_map/all_to_all | solution.py:56
  22.6 1.0 maximum_bitcast_fusion.1
  23.6 13.5 %all-to-all-start.2 = ((bf16[32,8,1536]{2,1,0:T(8,128)(2,1)}), bf16[32,8,1536]{2,1,0:T(8,128)(2,1)S(1)}, u32[]{:S(2)}, u32[]{:S(2)}) async-start(bf16[32,8,1536]{2,1,0:T(8,128)(2,1)} %maximum_bitcast_fusion.1), calls=%async_computation.2 | async-start | bytes 1572864 | tf_op jit(solution)/shard_map/all_to_all | solution.py:71
  37.0 1.9 %collective-permute-start.2 = (bf16[768,672]{0,1:T(8,128)(2,1)}, bf16[768,672]{0,1:T(8,128)(2,1)}, u32[]{:S(2)}, u32[]{:S(2)}) collective-permute-start(bf16[768,672]{0,1:T(8,128)(2,1)} %bitcast.10), channel_id=1, source_target_pairs={{0,128},{128,0},{1,129},{129,1},{2,130},{130,2},{3,131},{131,3},{4... | collective-permute-start | bytes 3096584 | tf_op jit(solution)/shard_map/ppermute | solution.py:49
  39.0 2.4 %collective-permute-start.3 = (bf16[768,672]{0,1:T(8,128)(2,1)}, bf16[768,672]{0,1:T(8,128)(2,1)S(1)}, u32[]{:S(2)}, u32[]{:S(2)}) collective-permute-start(bf16[768,672]{0,1:T(8,128)(2,1)} %bitcast.83), channel_id=1, source_target_pairs={{0,128},{128,0},{1,129},{129,1},{2,130},{130,2},{3,131},{131,3},{4... | collective-permute-start | bytes 3096584 | tf_op jit(solution)/shard_map/ppermute | solution.py:48
  42.0 0.9 maximum_bitcast_fusion
  42.9 14.9 %all-to-all-done.2 = bf16[32,8,1536]{2,1,0:T(8,128)(2,1)S(1)} async-done(((bf16[32,8,1536]{2,1,0:T(8,128)(2,1)}), bf16[32,8,1536]{2,1,0:T(8,128)(2,1)S(1)}, u32[]{:S(2)}, u32[]{:S(2)}) %all-to-all-start.2) | async-done | bytes 786464 | tf_op jit(solution)/shard_map/all_to_all | solution.py:71
  57.8 5.6 %all-to-all-start.1 = ((bf16[32,8,1536]{2,1,0:T(8,128)(2,1)}), bf16[32,8,1536]{2,1,0:T(8,128)(2,1)S(1)}, u32[]{:S(2)}, u32[]{:S(2)}) async-start(bf16[32,8,1536]{2,1,0:T(8,128)(2,1)} %maximum_bitcast_fusion), calls=%async_computation.1 | async-start | bytes 1572864 | tf_op jit(solution)/shard_map/all_to_all | solution.py:71
  63.4 1.9 %collective-permute-start = (bf16[672,768]{1,0:T(8,128)(2,1)}, bf16[672,768]{1,0:T(8,128)(2,1)}, u32[]{:S(2)}, u32[]{:S(2)}) collective-permute-start(bf16[672,768]{1,0:T(8,128)(2,1)} %bitcast.89), channel_id=1, source_target_pairs={{0,128},{128,0},{1,129},{129,1},{2,130},{130,2},{3,131},{131,3},{4... | collective-permute-start | bytes 3096584 | tf_op jit(solution)/shard_map/ppermute | solution.py:50
  65.3 1.7 fusion.13
  67.0 1.8 fusion.34
  69.3 1.3 fusion.35
  70.6 0.9 pad_maximum_fusion
  71.5 7.3 %collective-permute-start.4 = (bf16[1344,256]{1,0:T(8,128)(2,1)}, bf16[1344,256]{1,0:T(8,128)(2,1)}, u32[]{:S(2)}, u32[]{:S(2)}) collective-permute-start(bf16[1344,256]{1,0:T(8,128)(2,1)} %pad_maximum_fusion), channel_id=1, source_target_pairs={{0,256},{256,0},{1,257},{257,1},{2,258},{258,2},{3,259},{259,3},{4... | collective-permute-start | bytes 2064392 | tf_op jit(solution)/shard_map/ppermute | solution.py:79
  78.8 9.4 %all-to-all-done.1 = bf16[32,8,1536]{2,1,0:T(8,128)(2,1)S(1)} async-done(((bf16[32,8,1536]{2,1,0:T(8,128)(2,1)}), bf16[32,8,1536]{2,1,0:T(8,128)(2,1)S(1)}, u32[]{:S(2)}, u32[]{:S(2)}) %all-to-all-start.1) | async-done | bytes 786464 | tf_op jit(solution)/shard_map/all_to_all | solution.py:71
  88.2 1.7 fusion.17
  89.9 1.8 fusion.33
  91.7 28.3 %collective-permute-start.1 = (bf16[672,256]{1,0:T(8,128)(2,1)S(1)}, bf16[672,256]{1,0:T(8,128)(2,1)S(1)}, u32[]{:S(2)}, u32[]{:S(2)}) collective-permute-start(bf16[672,256]{1,0:T(8,128)(2,1)S(1)} %get-tuple-element.11), channel_id=1, source_target_pairs={{0,256},{256,0},{1,257},{257,1},{2,258},{258,2},{3,259},{259,3},{4... | collective-permute-start | bytes 1032200 | tf_op jit(solution)/shard_map/ppermute | solution.py:87
  120.0 8.0 %collective-permute-done.1 = bf16[672,256]{1,0:T(8,128)(2,1)S(1)} collective-permute-done((bf16[672,256]{1,0:T(8,128)(2,1)S(1)}, bf16[672,256]{1,0:T(8,128)(2,1)S(1)}, u32[]{:S(2)}, u32[]{:S(2)}) %collective-permute-start.1) | collective-permute-done | bytes 344096 | tf_op jit(solution)/shard_map/ppermute | solution.py:87
  128.0 2.3 %multiply_convert_fusion.2 = (bf16[672,256]{1,0:T(8,128)(2,1)S(1)}, bf16[672,256]{1,0:T(8,128)(2,1)S(1)}, bf16[672,256]{1,0:T(8,128)(2,1)}) fusion(f32[672,256]{1,0:T(8,128)S(1)} %get-tuple-element.12, bf16[672,256]{1,0:T(8,128)(2,1)S(1)} %collective-permute-done.1, f32[672,256]{1,0:T(8,128)S(1)} %get-tuple-element.14, f32[672,256]{1,0:T(8,128)S(1)} %copy-done.2, ...), kind=kLoop, calls=%fused_computation.26 | loop fusion | flops 3612672 | bytes 4128768 | tf_op jit(solution)/shard_map/convert_element_type | solution.py:97
  130.3 1.8 fusion.27
  132.6 1.7 fusion.36
  134.9 0.9 maximum_bitcast_fusion.2
  135.8 11.4 %all-to-all-start.3 = ((bf16[32,8,1536]{2,1,0:T(8,128)(2,1)}), bf16[32,8,1536]{2,1,0:T(8,128)(2,1)S(1)}, u32[]{:S(2)}, u32[]{:S(2)}) async-start(bf16[32,8,1536]{2,1,0:T(8,128)(2,1)} %maximum_bitcast_fusion.2), calls=%async_computation.3 | async-start | bytes 1572864 | tf_op jit(solution)/shard_map/all_to_all | solution.py:103
  147.2 1.9 %collective-permute-start.6 = (bf16[256,768]{1,0:T(8,128)(2,1)S(1)}, bf16[256,768]{1,0:T(8,128)(2,1)S(1)}, u32[]{:S(2)}, u32[]{:S(2)}) collective-permute-start(bf16[256,768]{1,0:T(8,128)(2,1)S(1)} %slice.74), channel_id=1, source_target_pairs={{0,128},{128,0},{1,129},{129,1},{2,130},{130,2},{3,131},{131,3},{4... | collective-permute-start | bytes 1179656 | tf_op jit(solution)/shard_map/ppermute | solution.py:83
  149.2 2.4 %collective-permute-start.5 = (bf16[672,256]{1,0:T(8,128)(2,1)S(1)}, bf16[672,256]{1,0:T(8,128)(2,1)}, u32[]{:S(2)}, u32[]{:S(2)}) collective-permute-start(bf16[672,256]{1,0:T(8,128)(2,1)S(1)} %copy-done.3), channel_id=1, source_target_pairs={{0,128},{128,0},{1,129},{129,1},{2,130},{130,2},{3,131},{131,3},{4... | collective-permute-start | bytes 1032200 | tf_op jit(solution)/shard_map/ppermute | solution.py:94
  151.6 13.4 %all-to-all-done.3 = bf16[32,8,1536]{2,1,0:T(8,128)(2,1)S(1)} async-done(((bf16[32,8,1536]{2,1,0:T(8,128)(2,1)}), bf16[32,8,1536]{2,1,0:T(8,128)(2,1)S(1)}, u32[]{:S(2)}, u32[]{:S(2)}) %all-to-all-start.3) | async-done | bytes 786464 | tf_op jit(solution)/shard_map/all_to_all | solution.py:103
  166.9 7.8 %all-to-all-start.4 = ((bf16[8,24,384]{2,1,0:T(8,128)(2,1)}), bf16[8,24,384]{2,1,0:T(8,128)(2,1)S(1)}, u32[]{:S(2)}, u32[]{:S(2)}) async-start(bf16[8,24,384]{2,1,0:T(8,128)(2,1)} %bitcast.24), calls=%async_computation.4 | async-start | bytes 294912 | tf_op jit(solution)/shard_map/all_to_all | solution.py:108
  175.1 2.4 %fusion.2 = bf16[1,672,768]{2,1,0:T(8,128)(2,1)} fusion(f32[672,768]{1,0:T(8,128)S(1)} %fusion.15, bf16[672,256]{1,0:T(8,128)(2,1)} %collective-permute-done.5, bf16[256,768]{1,0:T(8,128)(2,1)S(1)} %collective-permute-done.6), kind=kOutput, calls=%fused_computation.7 | convolution fusion | flops 265273344 | bytes 3833856 | tf_op jit(solution)/shard_map/dot_general | solution.py:32
  177.5 6.4 %all-to-all-done.4 = bf16[8,24,384]{2,1,0:T(8,128)(2,1)S(1)} async-done(((bf16[8,24,384]{2,1,0:T(8,128)(2,1)}), bf16[8,24,384]{2,1,0:T(8,128)(2,1)S(1)}, u32[]{:S(2)}, u32[]{:S(2)}) %all-to-all-start.4) | async-done | bytes 147488 | tf_op jit(solution)/shard_map/all_to_all | solution.py:108
  (45 shorter events, 9.6 us)
Async XLA Ops:
  2.1 19.7 %all-to-all-start = ((bf16[8,48,384]{2,1,0:T(8,128)(2,1)}), bf16[8,48,384]{2,1,0:T(8,128)(2,1)S(1)}, u32[]{:S(2)}, u32[]{:S(2)}) async-start(bf16[8,48,384]{2,1,0:T(8,128)(2,1)} %broadcast_in_dim.4), calls=%async_computation | async-start | bytes 589824 | tf_op jit(solution)/shard_map/all_to_all | solution.py:56
  23.6 34.2 %all-to-all-start.2 = ((bf16[32,8,1536]{2,1,0:T(8,128)(2,1)}), bf16[32,8,1536]{2,1,0:T(8,128)(2,1)S(1)}, u32[]{:S(2)}, u32[]{:S(2)}) async-start(bf16[32,8,1536]{2,1,0:T(8,128)(2,1)} %maximum_bitcast_fusion.1), calls=%async_computation.2 | async-start | bytes 1572864 | tf_op jit(solution)/shard_map/all_to_all | solution.py:71
  37.0 30.0 %collective-permute-start.2 = (bf16[768,672]{0,1:T(8,128)(2,1)}, bf16[768,672]{0,1:T(8,128)(2,1)}, u32[]{:S(2)}, u32[]{:S(2)}) collective-permute-start(bf16[768,672]{0,1:T(8,128)(2,1)} %bitcast.10), channel_id=1, source_target_pairs={{0,128},{128,0},{1,129},{129,1},{2,130},{130,2},{3,131},{131,3},{4... | collective-permute-start | bytes 3096584 | tf_op jit(solution)/shard_map/ppermute | solution.py:49
  39.0 30.3 %collective-permute-start.3 = (bf16[768,672]{0,1:T(8,128)(2,1)}, bf16[768,672]{0,1:T(8,128)(2,1)S(1)}, u32[]{:S(2)}, u32[]{:S(2)}) collective-permute-start(bf16[768,672]{0,1:T(8,128)(2,1)} %bitcast.83), channel_id=1, source_target_pairs={{0,128},{128,0},{1,129},{129,1},{2,130},{130,2},{3,131},{131,3},{4... | collective-permute-start | bytes 3096584 | tf_op jit(solution)/shard_map/ppermute | solution.py:48
  57.8 30.4 %all-to-all-start.1 = ((bf16[32,8,1536]{2,1,0:T(8,128)(2,1)}), bf16[32,8,1536]{2,1,0:T(8,128)(2,1)S(1)}, u32[]{:S(2)}, u32[]{:S(2)}) async-start(bf16[32,8,1536]{2,1,0:T(8,128)(2,1)} %maximum_bitcast_fusion), calls=%async_computation.1 | async-start | bytes 1572864 | tf_op jit(solution)/shard_map/all_to_all | solution.py:71
  63.4 26.5 %collective-permute-start = (bf16[672,768]{1,0:T(8,128)(2,1)}, bf16[672,768]{1,0:T(8,128)(2,1)}, u32[]{:S(2)}, u32[]{:S(2)}) collective-permute-start(bf16[672,768]{1,0:T(8,128)(2,1)} %bitcast.89), channel_id=1, source_target_pairs={{0,128},{128,0},{1,129},{129,1},{2,130},{130,2},{3,131},{131,3},{4... | collective-permute-start | bytes 3096584 | tf_op jit(solution)/shard_map/ppermute | solution.py:50
  67.0 1.8 copy-start
  71.5 56.5 %collective-permute-start.4 = (bf16[1344,256]{1,0:T(8,128)(2,1)}, bf16[1344,256]{1,0:T(8,128)(2,1)}, u32[]{:S(2)}, u32[]{:S(2)}) collective-permute-start(bf16[1344,256]{1,0:T(8,128)(2,1)} %pad_maximum_fusion), channel_id=1, source_target_pairs={{0,256},{256,0},{1,257},{257,1},{2,258},{258,2},{3,259},{259,3},{4... | collective-permute-start | bytes 2064392 | tf_op jit(solution)/shard_map/ppermute | solution.py:79
  89.9 38.1 %copy-start.2 = (f32[672,256]{1,0:T(8,128)S(1)}, f32[672,256]{1,0:T(8,128)}, u32[]{:S(2)}) copy-start(f32[672,256]{1,0:T(8,128)} %get-tuple-element.16) | copy-start | bytes 2064388
  91.7 36.3 %collective-permute-start.1 = (bf16[672,256]{1,0:T(8,128)(2,1)S(1)}, bf16[672,256]{1,0:T(8,128)(2,1)S(1)}, u32[]{:S(2)}, u32[]{:S(2)}) collective-permute-start(bf16[672,256]{1,0:T(8,128)(2,1)S(1)} %get-tuple-element.11), channel_id=1, source_target_pairs={{0,256},{256,0},{1,257},{257,1},{2,258},{258,2},{3,259},{259,3},{4... | collective-permute-start | bytes 1032200 | tf_op jit(solution)/shard_map/ppermute | solution.py:87
  130.3 1.8 copy-start.1
  135.8 13.4 %copy-start.3 = (bf16[672,256]{1,0:T(8,128)(2,1)S(1)}, bf16[672,256]{1,0:T(8,128)(2,1)}, u32[]{:S(2)}) copy-start(bf16[672,256]{1,0:T(8,128)(2,1)} %get-tuple-element.6) | copy-start | bytes 1032196
  135.8 29.2 %all-to-all-start.3 = ((bf16[32,8,1536]{2,1,0:T(8,128)(2,1)}), bf16[32,8,1536]{2,1,0:T(8,128)(2,1)S(1)}, u32[]{:S(2)}, u32[]{:S(2)}) async-start(bf16[32,8,1536]{2,1,0:T(8,128)(2,1)} %maximum_bitcast_fusion.2), calls=%async_computation.3 | async-start | bytes 1572864 | tf_op jit(solution)/shard_map/all_to_all | solution.py:103
  147.2 27.9 %collective-permute-start.6 = (bf16[256,768]{1,0:T(8,128)(2,1)S(1)}, bf16[256,768]{1,0:T(8,128)(2,1)S(1)}, u32[]{:S(2)}, u32[]{:S(2)}) collective-permute-start(bf16[256,768]{1,0:T(8,128)(2,1)S(1)} %slice.74), channel_id=1, source_target_pairs={{0,128},{128,0},{1,129},{129,1},{2,130},{130,2},{3,131},{131,3},{4... | collective-permute-start | bytes 1179656 | tf_op jit(solution)/shard_map/ppermute | solution.py:83
  149.2 25.9 %collective-permute-start.5 = (bf16[672,256]{1,0:T(8,128)(2,1)S(1)}, bf16[672,256]{1,0:T(8,128)(2,1)}, u32[]{:S(2)}, u32[]{:S(2)}) collective-permute-start(bf16[672,256]{1,0:T(8,128)(2,1)S(1)} %copy-done.3), channel_id=1, source_target_pairs={{0,128},{128,0},{1,129},{129,1},{2,130},{130,2},{3,131},{131,3},{4... | collective-permute-start | bytes 1032200 | tf_op jit(solution)/shard_map/ppermute | solution.py:94
  166.9 17.1 %all-to-all-start.4 = ((bf16[8,24,384]{2,1,0:T(8,128)(2,1)}), bf16[8,24,384]{2,1,0:T(8,128)(2,1)S(1)}, u32[]{:S(2)}, u32[]{:S(2)}) async-start(bf16[8,24,384]{2,1,0:T(8,128)(2,1)} %bitcast.24), calls=%async_computation.4 | async-start | bytes 294912 | tf_op jit(solution)/shard_map/all_to_all | solution.py:108

commit v2 on v1

v2 whole, which is shorter than its diff:
```python
import jax
import jax.numpy as jnp
from jax import lax
from jax.experimental import pallas as pl
from jax.experimental.pallas import tpu as pltpu
from jax.sharding import Mesh, PartitionSpec as P

CAP = 8
BF16 = jnp.bfloat16
F32 = jnp.float32
AXES = ("z_hi", "core", "z_lo", "x", "tensor")
BLOCKS = ("z_hi", "core", "z_lo", "x")
EXPERT = ("z_lo", "x")
SIDES = ("z_hi", "z_lo", "x")
SWAP = [(0, 1), (1, 0)]


def route_tables(expert_ids, route_weight, experts, capacity):
    onehot = (expert_ids[:, :, None] == jnp.arange(experts, dtype=jnp.int32)[None, None, :]).astype(
        jnp.int32
    )
    per_token = jnp.sum(onehot, axis=1)
    before = jnp.cumsum(per_token, axis=0) - per_token
    slot = jnp.sum(onehot * before[:, None, :], axis=2)
    target = expert_ids * capacity + slot
    places = jnp.arange(experts * capacity, dtype=jnp.int32)
    match = (target[:, :, None] == places[None, None, :]).astype(F32)
    select = jnp.sum(match, axis=1).astype(BF16)
    slot_weight = jnp.sum(match * route_weight[:, :, None], axis=(0, 1))
    return (select, slot_weight)


def dot(a, b, ca, cb):
    return lax.dot_general(a, b, (((ca,), (cb,)), ((), ())), preferred_element_type=F32)


def order_quarters(value, axis):
    shape = value.shape
    halves = value.reshape(shape[:axis] + (2, 2, shape[axis] // 4) + shape[axis + 1 :])
    flipped = jnp.flip(halves, axis=axis + 1)
    return jnp.where(lax.axis_index("core") == 0, halves, flipped).reshape(shape)


def params():
    return pltpu.CompilerParams(vmem_limit_bytes=40 * 1024 * 1024)


def cost(flops, moved):
    return pl.CostEstimate(flops=flops, bytes_accessed=moved, transcendentals=0)


def gate_up_body(own_gate, far_gate, own_up, far_up, own_x, far_x, exact, rounded):
    for i, (own, far) in enumerate(((own_gate, far_gate), (own_up, far_up))):
        value = dot(own[...], own_x[...], 1, 1) + dot(far[...], far_x[...], 1, 1)
        exact[i] = value
        rounded[i] = value.astype(BF16)


def gate_up_product(own_gate, far_gate, own_up, far_up, rows):
    hidden, quarter = own_gate.shape
    count = rows.shape[0]
    step = hidden // 3
    weight = pl.BlockSpec((step, quarter), lambda i: (i, 0))
    out = pl.BlockSpec((2, step, count), lambda i: (0, i, 0))
    return pl.pallas_call(
        gate_up_body,
        grid=(3,),
        in_specs=[weight] * 4
        + [
            pl.BlockSpec((count, quarter), lambda i: (0, 0)),
            pl.BlockSpec((count, quarter), lambda i: (0, 1)),
        ],
        out_specs=[out, out],
        out_shape=[
            jax.ShapeDtypeStruct((2, hidden, count), F32),
            jax.ShapeDtypeStruct((2, hidden, count), BF16),
        ],
        compiler_params=params(),
        cost_estimate=cost(8 * hidden * quarter * count, 8 * hidden * quarter),
    )(own_gate, far_gate, own_up, far_up, rows, rows)


def hidden_grad_body(own_down, far_down, own_dy, far_dy, exact, rounded):
    value = dot(own_down[...], own_dy[...], 1, 0) + dot(far_down[...], far_dy[...], 1, 0)
    exact[...] = value
    rounded[...] = value.astype(BF16)


def hidden_grad_product(own_down, far_down, columns):
    hidden, quarter = own_down.shape
    count = columns.shape[1]
    step = hidden // 3
    weight = pl.BlockSpec((step, quarter), lambda i: (i, 0))
    out = pl.BlockSpec((step, count), lambda i: (i, 0))
    return pl.pallas_call(
        hidden_grad_body,
        grid=(3,),
        in_specs=[weight] * 2
        + [
            pl.BlockSpec((quarter, count), lambda i: (0, 0)),
            pl.BlockSpec((quarter, count), lambda i: (1, 0)),
        ],
        out_specs=[out, out],
        out_shape=[
            jax.ShapeDtypeStruct((hidden, count), F32),
            jax.ShapeDtypeStruct((hidden, count), BF16),
        ],
        compiler_params=params(),
        cost_estimate=cost(4 * hidden * quarter * count, 4 * hidden * quarter),
    )(own_down, far_down, columns, columns)


def row_grad_body(
    exact, crossed, slope, active, own_gate, far_gate, own_up, far_up, out, own_sum, far_sum
):
    @pl.when(pl.program_id(0) == 0)
    def _():
        own_sum[...] = jnp.zeros_like(own_sum)
        far_sum[...] = jnp.zeros_like(far_sum)

    grad = exact[...] + crossed[...].astype(F32)
    gate_grad = (grad * slope[...]).astype(BF16)
    up_grad = (grad * active[...]).astype(BF16)
    own_sum[...] += dot(gate_grad, own_gate[...], 0, 0) + dot(up_grad, own_up[...], 0, 0)
    far_sum[...] += dot(gate_grad, far_gate[...], 0, 0) + dot(up_grad, far_up[...], 0, 0)

    @pl.when(pl.program_id(0) == pl.num_programs(0) - 1)
    def _():
        quarter = own_sum.shape[1]
        out[:, :quarter] = own_sum[...].astype(BF16)
        out[:, quarter:] = far_sum[...].astype(BF16)


def row_grad_product(exact, crossed, slope, active, own_gate, far_gate, own_up, far_up):
    hidden, quarter = own_gate.shape
    count = exact.shape[1]
    step = hidden // 3
    weight = pl.BlockSpec((step, quarter), lambda i: (i, 0))
    value = pl.BlockSpec((step, count), lambda i: (i, 0))
    return pl.pallas_call(
        row_grad_body,
        grid=(3,),
        in_specs=[value] * 4 + [weight] * 4,
        out_specs=pl.BlockSpec((count, 2 * quarter), lambda i: (0, 0)),
        out_shape=jax.ShapeDtypeStruct((count, 2 * quarter), BF16),
        scratch_shapes=[pltpu.VMEM((count, quarter), F32)] * 2,
        compiler_params=params(),
        cost_estimate=cost(8 * hidden * quarter * count, 8 * hidden * quarter),
    )(exact, crossed, slope, active, own_gate, far_gate, own_up, far_up)


def per_device(x_rows, cotangent, expert_ids, route_weight, gate_weight, up_weight, down_weight):
    tensor = lax.axis_size("tensor")
    experts = lax.axis_size(EXPERT)
    tokens, piece = x_rows.shape
    places = experts * CAP
    half = gate_weight.shape[1] * 2
    chunk = half // tensor
    own_gate, own_up, own_down = gate_weight[0].T, up_weight[0].T, down_weight[0]

    both = jnp.concatenate([x_rows, cotangent], axis=0)
    both = lax.all_to_all(
        jnp.broadcast_to(both[None], (tensor,) + both.shape), "tensor", 0, 0, tiled=True
    )
    select, slot_weight = route_tables(expert_ids, route_weight, experts, CAP)
    far_gate, far_up, far_down = (
        lax.ppermute(own_gate, "core", SWAP),
        lax.ppermute(own_up, "core", SWAP),
        lax.ppermute(own_down, "core", SWAP),
    )

    both = jnp.transpose(order_quarters(both, 0), (1, 0, 2)).reshape(2 * tokens, 2 * half)
    turn = lax.axis_index("tensor")
    sent = []
    for z in range(2):
        part = both[:, z * half : (z + 1) * half]
        dy = lax.dynamic_slice_in_dim(part[tokens:], turn * chunk, chunk, axis=1)
        dy = dot(select, dy, 0, 0) * slot_weight[:, None]
        dy = jnp.pad(dy, ((0, 0), (0, 256 - chunk)))
        sent.append(
            jnp.concatenate([dot(select, part[:tokens], 0, 0).astype(BF16), dy.astype(BF16)], axis=1)
        )
    sent = jnp.stack(sent).reshape(2 * experts, CAP, half + 256)
    got = lax.all_to_all(sent, SIDES, 0, 0, tiled=True).reshape(2 * places, half + 256)

    gate_up, gate_up_sent = gate_up_product(own_gate, far_gate, own_up, far_up, got)
    crossed = lax.ppermute(gate_up_sent, "z_hi", SWAP)
    got_dy = lax.all_gather(got[:, half : half + chunk].T, "tensor", axis=0, tiled=True)
    hidden_grad, hidden_grad_sent = hidden_grad_product(own_down, far_down, got_dy)
    crossed_grad = lax.ppermute(hidden_grad_sent, "z_hi", SWAP)
    swapped_dy = lax.ppermute(got_dy[half // 2 :], "core", SWAP)

    gate_up = gate_up + crossed.astype(F32)
    gate, up = gate_up[0], gate_up[1]
    sigma = jax.nn.sigmoid(gate)
    active = gate * sigma
    hidden = (active * up).astype(BF16)
    swapped_hidden = lax.ppermute(hidden, "core", SWAP)
    slope = up * sigma * (1.0 + gate * (1.0 - sigma))

    term = row_grad_product(
        hidden_grad, crossed_grad, slope, active, own_gate, far_gate, own_up, far_up
    )
    returned = lax.all_to_all(
        term.reshape(2 * experts, CAP, half), SIDES, 0, 0, tiled=True
    ).reshape(2, places, half)
    mixed = jnp.concatenate([dot(select, returned[z], 1, 0) for z in range(2)], axis=1)
    mixed = jnp.transpose(mixed.astype(BF16).reshape(tokens, tensor, piece), (1, 0, 2))
    mixed = lax.all_to_all(order_quarters(mixed, 0), "tensor", 0, 0, tiled=True)
    input_grad = jnp.sum(mixed.astype(F32), axis=0).astype(BF16)

    down_grad = dot(hidden, got_dy[: half // 2], 1, 1) + dot(swapped_hidden, swapped_dy, 1, 1)
    return (input_grad, down_grad.astype(BF16)[None])


def solution(mesh):
    fine = Mesh(mesh.devices.reshape(2, 2, 4, 4, 8), AXES)
    placed = (
        P(BLOCKS, "tensor"),
        P(BLOCKS, "tensor"),
        P(BLOCKS, None),
        P(BLOCKS, None),
        P(EXPERT, ("z_hi", "core"), "tensor"),
        P(EXPERT, ("z_hi", "core"), "tensor"),
        P(EXPERT, "tensor", ("z_hi", "core")),
    )
    return jax.shard_map(
        per_device,
        mesh=fine,
        in_specs=placed,
        out_specs=(P(BLOCKS, "tensor"), P(EXPERT, "tensor", ("z_hi", "core"))),
        check_vma=False,
    )
```

time: 186 us -> 163 us (0.88)
  starting transfers between devices: 91.5 us -> 56.1 us
  blocking collectives: 0 us -> 26 us
  matrix products: 17.8 us -> 4.67 us
  waiting for transfers between devices: 61.6 us -> 48.6 us
  local copies, waits for them, and re-layouts: 1.57 us -> 10.2 us
  Pallas kernels: 0 us -> 7.49 us
  other arithmetic: 11.1 us -> 7.72 us
    all_gather x0 -> x1, blocking collectives: none -> 26 us  [per_device(): lax.all_gather(got[:, half:half + chunk].T, 'tensor', axis=0, tiled=True)]
    ppermute x3, starting transfers between devices: 37.5 us -> 11.7 us  [the longest x1 6.47 us: per_device(): crossed_grad = lax.ppermute(hidden_grad_sent, 'z_hi', SWAP)]
    dot_general x18 -> x8, matrix products: 17.8 us -> 4.67 us  [dot(): lax.dot_general(a, b, (((ca,), (cb,)), ((), ())), preferred_element_type=...]
    all_to_all x3 -> x2, waiting for transfers between devices: 37.7 us -> 25.7 us  [the longest x1 15.3 us: per_device(): lax.all_to_all(sent, SIDES, 0, 0, tiled=True)]
    unnamed x10 -> x27, local copies, waits for them, and re-layouts: 0.06 us -> 7.91 us
    pallas_call x0 -> x3, Pallas kernels: none -> 7.49 us  [the longest x1 2.78 us: gate_up_product(): pl.pallas_call(gate_up_body, grid=(3,), in_specs=[weight] * 4 + [pl.Block...]
    all_to_all x3 -> x2, starting transfers between devices: 30.4 us -> 24.4 us  [the longest x1 13.6 us: per_device(): lax.all_to_all(sent, SIDES, 0, 0, tiled=True)]
    all_to_all x1, starting transfers between devices: 7.81 us -> 4.18 us  [per_device(): mixed = lax.all_to_all(order_quarters(mixed, 0), 'tensor', 0, 0, tiled=True)]
  transfers between devices with their start and end apart: 12 -> 11, of which waited for: 6 -> 5; matrix products, arithmetic and copies ran while one was open for 10% -> 6% of each run, Pallas kernels for 0% -> 3%
where the time goes in v2:
time: 163 us; the launch traced here: 162 us
  starting transfers between devices  56.1 us (34%)
  waiting for transfers between devices  48.6 us (30%)
  blocking collectives  26 us (16%)
  local copies, waits for them, and re-layouts  10.2 us (6%)
  other arithmetic  7.72 us (5%)
  Pallas kernels  7.49 us (5%)
  matrix products  4.67 us (3%)
    all_gather x1, blocking collectives, per_device(): lax.all_gather(got[:, half:half + chunk].T, 'tensor', axis=0, tiled=True)  26 us
    all_to_all x1, waiting for transfers between devices, per_device(): lax.all_to_all(sent, SIDES, 0, 0, tiled=True)  15.3 us
    all_to_all x1, starting transfers between devices, per_device(): lax.all_to_all(sent, SIDES, 0, 0, tiled=True)  13.6 us
    all_to_all x1, starting transfers between devices, per_device(): lax.all_to_all(term.reshape(2 * experts, CAP, half), SIDES, 0, 0, tiled=T...  10.8 us
    all_to_all x1, waiting for transfers between devices, per_device(): lax.all_to_all(term.reshape(2 * experts, CAP, half), SIDES, 0, 0, tiled=T...  10.3 us
    all_to_all x1, waiting for transfers between devices, per_device(): lax.all_to_all(jnp.broadcast_to(both[None], (tensor,) + both.shape), 'ten...  9.51 us
    unnamed x27, local copies, waits for them, and re-layouts  7.91 us
    all_to_all x1, starting transfers between devices, per_device(): lax.all_to_all(jnp.broadcast_to(both[None], (tensor,) + both.shape), 'ten...  7.1 us
  transfers between devices with their start and end apart: 11, of which 5 were waited for; matrix products, arithmetic and copies ran while one was open for 6% of the time, Pallas kernels for 3%

profile of v2, /device:TPU:2, one launch (start us, length us, event | category | flops | bytes accessed | tf_op | source)
XLA Modules:
  0.0 161.7 jit_solution(9120889220235290947)
XLA Ops:
  2.1 7.1 %all-to-all-start = ((bf16[8,48,384]{2,1,0:T(8,128)(2,1)}), bf16[8,48,384]{2,1,0:T(8,128)(2,1)S(1)}, u32[]{:S(2)}, u32[]{:S(2)}) async-start(bf16[8,48,384]{2,1,0:T(8,128)(2,1)} %broadcast_in_dim.4), calls=%async_computation | async-start | bytes 589824 | tf_op jit(solution)/shard_map/all_to_all | solution.py:162
  11.5 0.8 select_reduce_fusion
  12.3 9.5 %all-to-all-done = bf16[8,48,384]{2,1,0:T(8,128)(2,1)S(1)} async-done(((bf16[8,48,384]{2,1,0:T(8,128)(2,1)}), bf16[8,48,384]{2,1,0:T(8,128)(2,1)S(1)}, u32[]{:S(2)}, u32[]{:S(2)}) %all-to-all-start) | async-done | bytes 294944 | tf_op jit(solution)/shard_map/all_to_all | solution.py:162
  23.4 1.0 pad_maximum_fusion
  24.4 13.6 %all-to-all-start.1 = ((bf16[32,8,1792]{2,1,0:T(8,128)(2,1)}), bf16[32,8,1792]{2,1,0:T(8,128)(2,1)S(1)}, u32[]{:S(2)}, u32[]{:S(2)}) async-start(bf16[32,8,1792]{2,1,0:T(8,128)(2,1)} %bitcast.79), calls=%async_computation.1 | async-start | bytes 1835008 | tf_op jit(solution)/shard_map/all_to_all | solution.py:184
  38.1 1.9 %collective-permute-start.2 = (bf16[672,768]{1,0:T(8,128)(2,1)S(1)}, bf16[672,768]{1,0:T(8,128)(2,1)S(1)}, u32[]{:S(2)}, u32[]{:S(2)}) collective-permute-start(bf16[672,768]{1,0:T(8,128)(2,1)S(1)} %bitcast.70), channel_id=1, source_target_pairs={{0,128},{128,0},{1,129},{129,1},{2,130},{130,2},{3,131},{131,3},{4... | collective-permute-start | bytes 3096584 | tf_op jit(solution)/shard_map/ppermute | solution.py:167
  40.0 2.4 %collective-permute-start.3 = (bf16[672,768]{1,0:T(8,128)(2,1)S(1)}, bf16[672,768]{1,0:T(8,128)(2,1)S(1)}, u32[]{:S(2)}, u32[]{:S(2)}) collective-permute-start(bf16[672,768]{1,0:T(8,128)(2,1)S(1)} %bitcast.73), channel_id=1, source_target_pairs={{0,128},{128,0},{1,129},{129,1},{2,130},{130,2},{3,131},{131,3},{4... | collective-permute-start | bytes 3096584 | tf_op jit(solution)/shard_map/ppermute | solution.py:168
  42.4 1.9 %collective-permute-start = (bf16[672,768]{1,0:T(8,128)(2,1)}, bf16[672,768]{1,0:T(8,128)(2,1)}, u32[]{:S(2)}, u32[]{:S(2)}) collective-permute-start(bf16[672,768]{1,0:T(8,128)(2,1)} %bitcast.77), channel_id=1, source_target_pairs={{0,128},{128,0},{1,129},{129,1},{2,130},{130,2},{3,131},{131,3},{4... | collective-permute-start | bytes 3096584 | tf_op jit(solution)/shard_map/ppermute | solution.py:169
  44.4 1.0 copy-done.2
  45.3 1.0 copy-done.5
  46.3 15.3 %all-to-all-done.1 = bf16[32,8,1792]{2,1,0:T(8,128)(2,1)S(1)} async-done(((bf16[32,8,1792]{2,1,0:T(8,128)(2,1)}), bf16[32,8,1792]{2,1,0:T(8,128)(2,1)S(1)}, u32[]{:S(2)}, u32[]{:S(2)}) %all-to-all-start.1) | async-done | bytes 917536 | tf_op jit(solution)/shard_map/all_to_all | solution.py:184
  61.6 1.2 copy-done.3
  62.8 1.2 copy-done.6
  64.1 2.8 %shard_map.87 = (f32[2,672,256]{2,1,0:T(8,128)S(1)}, bf16[2,672,256]{2,1,0:T(8,128)(2,1)}) custom-call(bf16[672,768]{1,0:T(8,128)(2,1)S(1)} %bitcast.71, bf16[672,768]{1,0:T(8,128)(2,1)S(1)} %copy-done.3, bf16[672,768]{1,0:T(8,128)(2,1)S(1)} %bitcast.74, bf16[672,768]{1,0:T(8,128)(2,1)S(1)} %copy-done.6, bf16[256,1792]{1,0:T(8,128)(2,1)S(1)} %bitcast.67, ...), custom_call_target="tpu_custom_call" | custom-call | flops 1056964608 | bytes 4128768 | tf_op jit(solution)/shard_map/pallas_call | solution.py:65
  66.8 1.1 copy-done.9
  67.9 3.4 %collective-permute-start.4 = (bf16[2,672,256]{2,1,0:T(8,128)(2,1)}, bf16[2,672,256]{2,1,0:T(8,128)(2,1)}, u32[]{:S(2)}, u32[]{:S(2)}) collective-permute-start(bf16[2,672,256]{2,1,0:T(8,128)(2,1)} %get-tuple-element.9), channel_id=1, source_target_pairs={{0,256},{256,0},{1,257},{257,1},{2,258},{258,2},{3,259},{259,3},{4... | collective-permute-start | bytes 2064392 | tf_op jit(solution)/shard_map/ppermute | solution.py:187
  71.4 26.0 %all_gather.3.own_dy.far_dy = bf16[1536,256]{1,0:T(8,128)(2,1)S(1)} all-gather(bf16[192,256]{1,0:T(8,128)(2,1)S(1)} %copy.51), channel_id=1, replica_groups=mesh['z_hi'=2,'core'=2,'z_lo'=4,'x'=4,'tensor'=8] {'tensor'}, dimensions={0}, use_global_device_ids=true | all-gather | bytes 884736 | tf_op jit(solution)/shard_map/all_gather | solution.py:188
  97.5 1.3 copy-done.11
  98.8 2.7 %shard_map.86 = (f32[672,256]{1,0:T(8,128)S(1)}, bf16[672,256]{1,0:T(8,128)(2,1)S(1)}) custom-call(bf16[672,768]{1,0:T(8,128)(2,1)S(1)} %bitcast.78, bf16[672,768]{1,0:T(8,128)(2,1)} %collective-permute-done.far_down, bf16[1536,256]{1,0:T(8,128)(2,1)S(1)} %all_gather.3.own_dy.far_dy, bf16[1536,256]{1,0:T(8,128)(2,1)S(1)} %all_gather.3.own_dy.far_dy), custom_call_target="tpu_custom_call" | custom-call | flops 528482304 | bytes 2064384 | tf_op jit(solution)/shard_map/pallas_call | solution.py:95
  101.5 6.5 %collective-permute-start.1 = (bf16[672,256]{1,0:T(8,128)(2,1)S(1)}, bf16[672,256]{1,0:T(8,128)(2,1)S(1)}, u32[]{:S(2)}, u32[]{:S(2)}) collective-permute-start(bf16[672,256]{1,0:T(8,128)(2,1)S(1)} %get-tuple-element.7), channel_id=1, source_target_pairs={{0,256},{256,0},{1,257},{257,1},{2,258},{258,2},{3,259},{259,3},{4... | collective-permute-start | bytes 1032200 | tf_op jit(solution)/shard_map/ppermute | solution.py:190
  108.0 1.2 convert_add_fusion
  109.6 7.0 %collective-permute-done.1.crossed = bf16[672,256]{1,0:T(8,128)(2,1)S(1)} collective-permute-done((bf16[672,256]{1,0:T(8,128)(2,1)S(1)}, bf16[672,256]{1,0:T(8,128)(2,1)S(1)}, u32[]{:S(2)}, u32[]{:S(2)}) %collective-permute-start.1) | collective-permute-done | bytes 344096 | tf_op jit(solution)/shard_map/ppermute | solution.py:190
  116.6 2.0 %shard_map.88 = bf16[256,1536]{1,0:T(8,128)(2,1)S(1)} custom-call(f32[672,256]{1,0:T(8,128)S(1)} %get-tuple-element.6.exact, bf16[672,256]{1,0:T(8,128)(2,1)S(1)} %collective-permute-done.1.crossed, f32[672,256]{1,0:T(8,128)S(1)} %get-tuple-element.14.slope, f32[672,256]{1,0:T(8,128)S(1)} %get-tuple-element.13.active, bf16[672,768]{1,0:T(8,128)(2,1)S(1)} %bitcast.72, ...), custom_call_target="tpu_custom_call" | custom-call | flops 1056964608 | bytes 4128768 | tf_op jit(solution)/shard_map/pallas_call | solution.py:140
  118.6 0.9 copy-done.8
  119.5 10.8 %all-to-all-start.2 = ((bf16[32,8,1536]{2,1,0:T(8,128)(2,1)}), bf16[32,8,1536]{2,1,0:T(8,128)(2,1)S(1)}, u32[]{:S(2)}, u32[]{:S(2)}) async-start(bf16[32,8,1536]{2,1,0:T(8,128)(2,1)} %bitcast.76), calls=%async_computation.2 | async-start | bytes 1572864 | tf_op jit(solution)/shard_map/all_to_all | solution.py:204
  130.3 0.8 slice.62
  131.1 1.9 %collective-permute-start.6 = (bf16[768,256]{1,0:T(8,128)(2,1)}, bf16[768,256]{1,0:T(8,128)(2,1)S(1)}, u32[]{:S(2)}, u32[]{:S(2)}) collective-permute-start(bf16[768,256]{1,0:T(8,128)(2,1)} %slice.62), channel_id=1, source_target_pairs={{0,128},{128,0},{1,129},{129,1},{2,130},{130,2},{3,131},{131,3},{4... | collective-permute-start | bytes 1179656 | tf_op jit(solution)/shard_map/ppermute | solution.py:191
  133.0 2.4 %collective-permute-start.5 = (bf16[672,256]{1,0:T(8,128)(2,1)S(1)}, bf16[672,256]{1,0:T(8,128)(2,1)}, u32[]{:S(2)}, u32[]{:S(2)}) collective-permute-start(bf16[672,256]{1,0:T(8,128)(2,1)S(1)} %get-tuple-element.12), channel_id=1, source_target_pairs={{0,128},{128,0},{1,129},{129,1},{2,130},{130,2},{3,131},{131,3},{4... | collective-permute-start | bytes 1032200 | tf_op jit(solution)/shard_map/ppermute | solution.py:198
  135.4 10.3 %all-to-all-done.2 = bf16[32,8,1536]{2,1,0:T(8,128)(2,1)S(1)} async-done(((bf16[32,8,1536]{2,1,0:T(8,128)(2,1)}), bf16[32,8,1536]{2,1,0:T(8,128)(2,1)S(1)}, u32[]{:S(2)}, u32[]{:S(2)}) %all-to-all-start.2) | async-done | bytes 786464 | tf_op jit(solution)/shard_map/all_to_all | solution.py:204
  147.6 4.2 %all-to-all-start.3 = ((bf16[8,24,384]{2,1,0:T(8,128)(2,1)}), bf16[8,24,384]{2,1,0:T(8,128)(2,1)S(1)}, u32[]{:S(2)}, u32[]{:S(2)}) async-start(bf16[8,24,384]{2,1,0:T(8,128)(2,1)} %bitcast.28), calls=%async_computation.3 | async-start | bytes 294912 | tf_op jit(solution)/shard_map/all_to_all | solution.py:209
  152.3 2.4 %fusion = bf16[1,672,768]{2,1,0:T(8,128)(2,1)} fusion(f32[672,768]{1,0:T(8,128)S(1)} %fusion.10, bf16[672,256]{1,0:T(8,128)(2,1)} %collective-permute-done.5, bf16[768,256]{1,0:T(8,128)(2,1)S(1)} %collective-permute-done.6), kind=kOutput, calls=%fused_computation.4 | convolution fusion | flops 265273344 | bytes 3833856 | tf_op jit(solution)/shard_map/dot_general | solution.py:34
  154.7 6.4 %all-to-all-done.3 = bf16[8,24,384]{2,1,0:T(8,128)(2,1)S(1)} async-done(((bf16[8,24,384]{2,1,0:T(8,128)(2,1)}), bf16[8,24,384]{2,1,0:T(8,128)(2,1)S(1)}, u32[]{:S(2)}, u32[]{:S(2)}) %all-to-all-start.3) | async-done | bytes 147488 | tf_op jit(solution)/shard_map/all_to_all | solution.py:209
  (54 shorter events, 8.8 us)
Async XLA Ops:
  2.1 19.7 %all-to-all-start = ((bf16[8,48,384]{2,1,0:T(8,128)(2,1)}), bf16[8,48,384]{2,1,0:T(8,128)(2,1)S(1)}, u32[]{:S(2)}, u32[]{:S(2)}) async-start(bf16[8,48,384]{2,1,0:T(8,128)(2,1)} %broadcast_in_dim.4), calls=%async_computation | async-start | bytes 589824 | tf_op jit(solution)/shard_map/all_to_all | solution.py:162
  23.4 16.6 %copy-start.1 = (bf16[1,768,672]{1,2,0:T(8,128)(2,1)S(1)}, bf16[1,768,672]{1,2,0:T(8,128)(2,1)}, u32[]{:S(2)}) copy-start(bf16[1,768,672]{1,2,0:T(8,128)(2,1)} %param.12) | copy-start | bytes 3096580
  24.4 13.6 %copy-start = (bf16[1,768,672]{1,2,0:T(8,128)(2,1)S(1)}, bf16[1,768,672]{1,2,0:T(8,128)(2,1)}, u32[]{:S(2)}) copy-start(bf16[1,768,672]{1,2,0:T(8,128)(2,1)} %param.11) | copy-start | bytes 3096580
  24.4 37.2 %all-to-all-start.1 = ((bf16[32,8,1792]{2,1,0:T(8,128)(2,1)}), bf16[32,8,1792]{2,1,0:T(8,128)(2,1)S(1)}, u32[]{:S(2)}, u32[]{:S(2)}) async-start(bf16[32,8,1792]{2,1,0:T(8,128)(2,1)} %bitcast.79), calls=%async_computation.1 | async-start | bytes 1835008 | tf_op jit(solution)/shard_map/all_to_all | solution.py:184
  38.1 6.3 %collective-permute-start.2 = (bf16[672,768]{1,0:T(8,128)(2,1)S(1)}, bf16[672,768]{1,0:T(8,128)(2,1)S(1)}, u32[]{:S(2)}, u32[]{:S(2)}) collective-permute-start(bf16[672,768]{1,0:T(8,128)(2,1)S(1)} %bitcast.70), channel_id=1, source_target_pairs={{0,128},{128,0},{1,129},{129,1},{2,130},{130,2},{3,131},{131,3},{4... | collective-permute-start | bytes 3096584 | tf_op jit(solution)/shard_map/ppermute | solution.py:167
  40.0 5.3 %collective-permute-start.3 = (bf16[672,768]{1,0:T(8,128)(2,1)S(1)}, bf16[672,768]{1,0:T(8,128)(2,1)S(1)}, u32[]{:S(2)}, u32[]{:S(2)}) collective-permute-start(bf16[672,768]{1,0:T(8,128)(2,1)S(1)} %bitcast.73), channel_id=1, source_target_pairs={{0,128},{128,0},{1,129},{129,1},{2,130},{130,2},{3,131},{131,3},{4... | collective-permute-start | bytes 3096584 | tf_op jit(solution)/shard_map/ppermute | solution.py:168
  42.4 55.0 %collective-permute-start = (bf16[672,768]{1,0:T(8,128)(2,1)}, bf16[672,768]{1,0:T(8,128)(2,1)}, u32[]{:S(2)}, u32[]{:S(2)}) collective-permute-start(bf16[672,768]{1,0:T(8,128)(2,1)} %bitcast.77), channel_id=1, source_target_pairs={{0,128},{128,0},{1,129},{129,1},{2,130},{130,2},{3,131},{131,3},{4... | collective-permute-start | bytes 3096584 | tf_op jit(solution)/shard_map/ppermute | solution.py:169
  44.3 1.0 copy-start.2
  45.3 1.0 copy-start.5
  61.6 1.2 copy-start.3
  62.8 1.2 copy-start.6
  66.8 1.1 copy-start.9
  67.9 40.0 %collective-permute-start.4 = (bf16[2,672,256]{2,1,0:T(8,128)(2,1)}, bf16[2,672,256]{2,1,0:T(8,128)(2,1)}, u32[]{:S(2)}, u32[]{:S(2)}) collective-permute-start(bf16[2,672,256]{2,1,0:T(8,128)(2,1)} %get-tuple-element.9), channel_id=1, source_target_pairs={{0,256},{256,0},{1,257},{257,1},{2,258},{258,2},{3,259},{259,3},{4... | collective-permute-start | bytes 2064392 | tf_op jit(solution)/shard_map/ppermute | solution.py:187
  97.4 10.5 %copy-start.10 = (f32[2,672,256]{2,1,0:T(8,128)S(1)}, f32[2,672,256]{2,1,0:T(8,128)}, u32[]{:S(2)}) copy-start(f32[2,672,256]{2,1,0:T(8,128)} %copy-done.9) | copy-start | bytes 4128772
  97.5 1.3 copy-start.11
  101.5 15.1 %collective-permute-start.1 = (bf16[672,256]{1,0:T(8,128)(2,1)S(1)}, bf16[672,256]{1,0:T(8,128)(2,1)S(1)}, u32[]{:S(2)}, u32[]{:S(2)}) collective-permute-start(bf16[672,256]{1,0:T(8,128)(2,1)S(1)} %get-tuple-element.7), channel_id=1, source_target_pairs={{0,256},{256,0},{1,257},{257,1},{2,258},{258,2},{3,259},{259,3},{4... | collective-permute-start | bytes 1032200 | tf_op jit(solution)/shard_map/ppermute | solution.py:190
  109.2 7.4 %copy-start.4 = (bf16[672,768]{1,0:T(8,128)(2,1)S(1)}, bf16[672,768]{1,0:T(8,128)(2,1)}, u32[]{:S(2)}) copy-start(bf16[672,768]{1,0:T(8,128)(2,1)} %copy-done.2) | copy-start | bytes 3096580
  109.2 7.4 %copy-start.7 = (bf16[672,768]{1,0:T(8,128)(2,1)S(1)}, bf16[672,768]{1,0:T(8,128)(2,1)}, u32[]{:S(2)}) copy-start(bf16[672,768]{1,0:T(8,128)(2,1)} %copy-done.5) | copy-start | bytes 3096580
  118.6 0.9 copy-start.8
  119.5 26.2 %all-to-all-start.2 = ((bf16[32,8,1536]{2,1,0:T(8,128)(2,1)}), bf16[32,8,1536]{2,1,0:T(8,128)(2,1)S(1)}, u32[]{:S(2)}, u32[]{:S(2)}) async-start(bf16[32,8,1536]{2,1,0:T(8,128)(2,1)} %bitcast.76), calls=%async_computation.2 | async-start | bytes 1572864 | tf_op jit(solution)/shard_map/all_to_all | solution.py:204
  131.1 21.2 %collective-permute-start.6 = (bf16[768,256]{1,0:T(8,128)(2,1)}, bf16[768,256]{1,0:T(8,128)(2,1)S(1)}, u32[]{:S(2)}, u32[]{:S(2)}) collective-permute-start(bf16[768,256]{1,0:T(8,128)(2,1)} %slice.62), channel_id=1, source_target_pairs={{0,128},{128,0},{1,129},{129,1},{2,130},{130,2},{3,131},{131,3},{4... | collective-permute-start | bytes 1179656 | tf_op jit(solution)/shard_map/ppermute | solution.py:191
  133.0 19.3 %collective-permute-start.5 = (bf16[672,256]{1,0:T(8,128)(2,1)S(1)}, bf16[672,256]{1,0:T(8,128)(2,1)}, u32[]{:S(2)}, u32[]{:S(2)}) collective-permute-start(bf16[672,256]{1,0:T(8,128)(2,1)S(1)} %get-tuple-element.12), channel_id=1, source_target_pairs={{0,128},{128,0},{1,129},{129,1},{2,130},{130,2},{3,131},{131,3},{4... | collective-permute-start | bytes 1032200 | tf_op jit(solution)/shard_map/ppermute | solution.py:198
  147.6 13.4 %all-to-all-start.3 = ((bf16[8,24,384]{2,1,0:T(8,128)(2,1)}), bf16[8,24,384]{2,1,0:T(8,128)(2,1)S(1)}, u32[]{:S(2)}, u32[]{:S(2)}) async-start(bf16[8,24,384]{2,1,0:T(8,128)(2,1)} %bitcast.28), calls=%async_computation.3 | async-start | bytes 294912 | tf_op jit(solution)/shard_map/all_to_all | solution.py:209

commit v3 on v1

v3 whole, which is shorter than its diff:
```python
import functools

import jax
import jax.numpy as jnp
from jax import lax
from jax.experimental import pallas as pl
from jax.experimental.pallas import tpu as pltpu
from jax.sharding import Mesh, PartitionSpec as P

CAP = 8
BF16 = jnp.bfloat16
F32 = jnp.float32
AXES = ("z_hi", "core", "z_lo", "x", "tensor")
BLOCKS = ("z_hi", "core", "z_lo", "x")
EXPERT = ("z_lo", "x")
SIDES = ("z_hi", "z_lo", "x")
SWAP = [(0, 1), (1, 0)]


def route_tables(expert_ids, route_weight, experts, capacity):
    onehot = (expert_ids[:, :, None] == jnp.arange(experts, dtype=jnp.int32)[None, None, :]).astype(
        jnp.int32
    )
    per_token = jnp.sum(onehot, axis=1)
    before = jnp.cumsum(per_token, axis=0) - per_token
    slot = jnp.sum(onehot * before[:, None, :], axis=2)
    target = expert_ids * capacity + slot
    places = jnp.arange(experts * capacity, dtype=jnp.int32)
    select = jnp.sum((target[:, :, None] == places[None, None, :]).astype(F32), axis=1).astype(BF16)
    match = (target.T[None] == places[:, None, None]).astype(F32)
    gather = jnp.sum(match, axis=1).astype(BF16)
    slot_weight = jnp.sum(match * route_weight.T[None], axis=(1, 2))
    return (select, gather, slot_weight[:, None])


def dot(a, b, ca, cb):
    return lax.dot_general(a, b, (((ca,), (cb,)), ((), ())), preferred_element_type=F32)


def params():
    return pltpu.CompilerParams(vmem_limit_bytes=16 * 1024 * 1024)


def in_hbm(*arrays):
    return [pltpu.with_memory_space_constraint(array, pltpu.HBM) for array in arrays]


def in_vmem(*arrays):
    return [pltpu.with_memory_space_constraint(array, pltpu.VMEM) for array in arrays]


def cost(flops, moved):
    return pl.CostEstimate(flops=flops, bytes_accessed=moved, transcendentals=0)


def spread_body(x_rows, cotangent, out):
    tokens, piece = x_rows.shape
    half = piece // 2
    blank = jnp.zeros((tokens, out.shape[2] - piece - half), BF16)
    for j in range(2):
        part = jnp.concatenate([cotangent[:, j * half : (j + 1) * half], blank], axis=1)
        for i in range(j, out.shape[0], 2):
            out[i, :, :piece] = x_rows[...]
            out[i, :, piece:] = part


def spread(x_rows, cotangent, tensor):
    tokens, piece = x_rows.shape
    vmem = pl.BlockSpec(memory_space=pltpu.VMEM)
    return pl.pallas_call(
        spread_body,
        in_specs=[vmem] * 2,
        out_specs=vmem,
        out_shape=pltpu.HBM((tensor, tokens, piece + 256), BF16),
        compiler_params=params(),
        cost_estimate=cost(0, 600000),
    )(*in_hbm(x_rows, cotangent))


def dispatch_body(place, tokens, gather, slot_weight, out, held, leave):
    core, turn = place[0], place[1]
    piece = tokens.shape[2] - 256
    stores = []
    for z in range(2):
        for k in range(4):
            which = z * 4 + (core * 2 if k < 2 else 2 - core * 2) + k % 2
            part = dot(gather[...], tokens[which, :, :piece], 1, 0)
            held[z, :, k * piece : (k + 1) * piece] = part.astype(BF16)
        k = turn // 2
        which = z * 4 + jnp.where(k < 2, core * 2, 2 - core * 2) + k % 2
        dy = dot(gather[...], tokens[which, :, piece:], 1, 0) * slot_weight[...]
        held[z, :, 4 * piece :] = dy.astype(BF16)
        stores.append(pltpu.make_async_copy(held.at[z], out.at[z], leave.at[z]))
        stores[-1].start()
    for store in stores:
        store.wait()


def dispatch(place, tokens, gather, slot_weight):
    count = slot_weight.shape[0]
    vmem = pl.BlockSpec(memory_space=pltpu.VMEM)
    shape = (2, count, 4 * (tokens.shape[2] - 256) + 256)
    return pl.pallas_call(
        dispatch_body,
        in_specs=[pl.BlockSpec(memory_space=pltpu.SMEM), vmem, vmem, vmem],
        out_specs=pl.BlockSpec(memory_space=pl.ANY),
        out_shape=pltpu.HBM(shape, BF16),
        scratch_shapes=[pltpu.VMEM(shape, BF16), pltpu.SemaphoreType.DMA((2,))],
        compiler_params=params(),
        cost_estimate=cost(2 * 24 * 8 * 384 * 128, 1600000),
    )(place, tokens, gather, slot_weight)


def combine_body(place, returned, select, out):
    core = place[0]
    piece = out.shape[2]
    for z in range(2):
        for k in range(4):
            which = z * 4 + (core * 2 if k < 2 else 2 - core * 2) + k % 2
            part = returned[z, :, k * piece : (k + 1) * piece]
            out[which] = dot(select[...], part, 1, 0).astype(BF16)


def combine(place, returned, select, tensor):
    tokens = select.shape[0]
    vmem = pl.BlockSpec(memory_space=pltpu.VMEM)
    return pl.pallas_call(
        combine_body,
        in_specs=[pl.BlockSpec(memory_space=pltpu.SMEM), vmem, vmem],
        out_specs=vmem,
        out_shape=jax.ShapeDtypeStruct((tensor, tokens, 2 * returned.shape[2] // tensor), BF16),
        compiler_params=params(),
        cost_estimate=cost(2 * 24 * 128 * 3072, 1000000),
    )(place, returned, select)


def chunks(total, parts):
    step = total // parts
    return [pl.ds(i * step, step) for i in range(parts)]


def hold_body(*refs):
    count = len(refs) // 2
    for source, target in zip(refs[:count], refs[count:]):
        target[...] = source[...]


def hold(*arrays):
    vmem = pl.BlockSpec(memory_space=pltpu.VMEM)
    return pl.pallas_call(
        hold_body,
        in_specs=[vmem] * len(arrays),
        out_specs=[vmem] * len(arrays),
        out_shape=[pltpu.VMEM(array.shape, array.dtype) for array in arrays],
        compiler_params=params(),
        cost_estimate=cost(0, 2000000 * len(arrays)),
    )(*arrays)


def project_body(pairs, side, *refs):
    own, far, (act, out, fetched, partial, held, arrive, leave) = (
        refs[:pairs],
        refs[pairs : 2 * pairs],
        refs[2 * pairs :],
    )
    quarter = own[0].shape[1]
    pieces = chunks(held.shape[1], leave.shape[1])
    fetch_own = fetched.shape[0] == 2 * pairs
    sources = (list(own) if fetch_own else []) + list(far)
    loads = [
        [
            pltpu.make_async_copy(source.at[piece], fetched.at[p, piece], arrive.at[p, i])
            for i, piece in enumerate(pieces)
        ]
        for p, source in enumerate(sources)
    ]
    for group in loads:
        for load in group:
            load.start()
    near, away = pl.ds(0, quarter), pl.ds(quarter, quarter)
    near = act[:, near] if side == 1 else act[near]
    away = act[:, away] if side == 1 else act[away]
    for i, piece in enumerate(pieces):
        for p in range(pairs):
            if fetch_own:
                loads[p][i].wait()
            rows = fetched[p, piece] if fetch_own else own[p][piece]
            partial[p, piece] = dot(rows, near, 1, side)
    stores = []
    shift = pairs if fetch_own else 0
    for p in range(pairs):
        for i, piece in enumerate(pieces):
            loads[shift + p][i].wait()
            value = partial[p, piece] + dot(fetched[shift + p, piece], away, 1, side)
            held[p, piece] = value.astype(BF16)
            stores.append(
                pltpu.make_async_copy(held.at[p, piece], out.at[p, piece], leave.at[p, i])
            )
            stores[-1].start()
    for store in stores:
        store.wait()


def project(own, far, act, side, count, fetch_own):
    pairs = len(own)
    hidden, quarter = own[0].shape
    parts = 3
    vmem, hbm = pl.BlockSpec(memory_space=pltpu.VMEM), pl.BlockSpec(memory_space=pl.ANY)
    fetched = 2 * pairs if fetch_own else pairs
    return pl.pallas_call(
        functools.partial(project_body, pairs, side),
        in_specs=[hbm if fetch_own else vmem] * pairs + [hbm] * pairs + [vmem],
        out_specs=hbm,
        out_shape=pltpu.HBM((pairs, hidden, count), BF16),
        scratch_shapes=[
            pltpu.VMEM((fetched, hidden, quarter), BF16),
            pltpu.VMEM((pairs, hidden, count), F32),
            pltpu.VMEM((pairs, hidden, count), BF16),
            pltpu.SemaphoreType.DMA((fetched, parts)),
            pltpu.SemaphoreType.DMA((pairs, parts)),
        ],
        compiler_params=params(),
        cost_estimate=cost(4 * pairs * hidden * quarter * count, 4 * pairs * hidden * quarter),
    )(*(in_hbm if fetch_own else in_vmem)(*own), *in_hbm(*far), act)


def row_grad_body(
    kept, crossed, slope, active, own_gate, own_up, far_gate, far_up, out, held, leave
):
    quarter = own_gate.shape[1]
    parts = leave.shape[1]
    grad = kept[0].astype(F32) + crossed[0].astype(F32)
    gate_grad = (grad * slope[...]).T.astype(BF16)
    up_grad = (grad * active[...]).T.astype(BF16)
    stores = []
    for half, (gate, up) in enumerate(((own_gate, own_up), (far_gate, far_up))):
        for i, piece in enumerate(chunks(quarter, parts)):
            value = dot(gate_grad, gate[:, piece], 1, 0) + dot(up_grad, up[:, piece], 1, 0)
            where = pl.ds(half * quarter + i * (quarter // parts), quarter // parts)
            held[:, where] = value.astype(BF16)
            stores.append(
                pltpu.make_async_copy(held.at[:, where], out.at[:, where], leave.at[half, i])
            )
            stores[-1].start()
    for store in stores:
        store.wait()


def row_grad_product(kept, crossed, slope, active, weights):
    hidden, quarter = weights[0].shape
    count = kept.shape[2]
    parts = 3
    vmem = pl.BlockSpec(memory_space=pltpu.VMEM)
    return pl.pallas_call(
        row_grad_body,
        in_specs=[vmem] * 8,
        out_specs=pl.BlockSpec(memory_space=pl.ANY),
        out_shape=pltpu.HBM((count, 2 * quarter), BF16),
        scratch_shapes=[
            pltpu.VMEM((count, 2 * quarter), BF16),
            pltpu.SemaphoreType.DMA((2, parts)),
        ],
        compiler_params=params(),
        cost_estimate=cost(8 * hidden * quarter * count, 8 * hidden * quarter),
    )(*in_vmem(kept, crossed, slope, active, *weights))


def per_device(x_rows, cotangent, expert_ids, route_weight, gate_weight, up_weight, down_weight):
    tensor = lax.axis_size("tensor")
    experts = lax.axis_size(EXPERT)
    tokens, piece = x_rows.shape
    places = experts * CAP
    half = gate_weight.shape[1] * 2
    chunk = half // tensor
    own_gate, own_up, own_down = gate_weight[0].T, up_weight[0].T, down_weight[0]

    both = spread(x_rows, cotangent, tensor)
    both = lax.all_to_all(both, "tensor", 0, 0, tiled=True)
    select, gather, slot_weight = route_tables(expert_ids, route_weight, experts, CAP)
    place = jnp.stack([lax.axis_index("core"), lax.axis_index("tensor")]).astype(jnp.int32)
    far_gate, far_up, far_down = (
        lax.ppermute(own_gate, "core", SWAP),
        lax.ppermute(own_up, "core", SWAP),
        lax.ppermute(own_down, "core", SWAP),
    )

    sent = dispatch(place, both, gather, slot_weight).reshape(2 * experts, CAP, half + 256)
    got = lax.all_to_all(sent, SIDES, 0, 0, tiled=True).reshape(2 * places, half + 256)

    rows = 2 * places
    gate_up = project((own_gate, own_up), (far_gate, far_up), got, 1, rows, False)
    crossed = lax.ppermute(gate_up, "z_hi", SWAP)
    got_dy = lax.all_gather(got[:, half : half + chunk].T, "tensor", axis=0, tiled=True)
    hidden_grad = project((own_down,), (far_down,), got_dy, 0, rows, True)
    crossed_grad = lax.ppermute(hidden_grad, "z_hi", SWAP)
    swapped_dy = lax.ppermute(got_dy[half // 2 :], "core", SWAP)

    gate_up = gate_up.astype(F32) + crossed.astype(F32)
    gate, up = gate_up[0], gate_up[1]
    sigma = jax.nn.sigmoid(gate)
    active = gate * sigma
    hidden = (active * up).astype(BF16)
    swapped_hidden = lax.ppermute(hidden, "core", SWAP)
    slope = up * sigma * (1.0 + gate * (1.0 - sigma))

    far_gate, far_up, _ = lax.optimization_barrier((far_gate, far_up, crossed))
    far_gate, far_up = hold(*in_hbm(far_gate, far_up))
    term = row_grad_product(
        hidden_grad, crossed_grad, slope, active, (own_gate, own_up, far_gate, far_up)
    )
    returned = lax.all_to_all(
        term.reshape(2 * experts, CAP, half), SIDES, 0, 0, tiled=True
    ).reshape(2, places, half)
    mixed = combine(place, returned, select, tensor)
    mixed = lax.all_to_all(mixed, "tensor", 0, 0, tiled=True)
    input_grad = jnp.sum(mixed.astype(F32), axis=0).astype(BF16)

    down_grad = dot(hidden, got_dy[: half // 2], 1, 1) + dot(swapped_hidden, swapped_dy, 1, 1)
    return (input_grad, down_grad.astype(BF16)[None])


def solution(mesh):
    fine = Mesh(mesh.devices.reshape(2, 2, 4, 4, 8), AXES)
    placed = (
        P(BLOCKS, "tensor"),
        P(BLOCKS, "tensor"),
        P(BLOCKS, None),
        P(BLOCKS, None),
        P(EXPERT, ("z_hi", "core"), "tensor"),
        P(EXPERT, ("z_hi", "core"), "tensor"),
        P(EXPERT, "tensor", ("z_hi", "core")),
    )
    return jax.shard_map(
        per_device,
        mesh=fine,
        in_specs=placed,
        out_specs=(P(BLOCKS, "tensor"), P(EXPERT, "tensor", ("z_hi", "core"))),
        check_vma=False,
    )
```

time: 186 us -> 157 us (0.84)
  starting transfers between devices: 91.5 us -> 55.7 us
  blocking collectives: 0 us -> 26.2 us
  Pallas kernels: 0 us -> 16.1 us
  matrix products: 17.8 us -> 1.92 us
  waiting for transfers between devices: 61.6 us -> 48.6 us
  other arithmetic: 11.1 us -> 5.28 us
    all_gather x0 -> x1, blocking collectives: none -> 26.2 us  [per_device(): lax.all_gather(got[:, half:half + chunk].T, 'tensor', axis=0, tiled=True)]
    ppermute x3, starting transfers between devices: 37.5 us -> 11.7 us  [the longest x1 6.45 us: per_device(): crossed_grad = lax.ppermute(hidden_grad, 'z_hi', SWAP)]
    pallas_call x0 -> x7, Pallas kernels: none -> 16.1 us  [the longest x2 7.4 us: project(): pl.pallas_call(functools.partial(project_body, pairs, side), in_specs=[hb...]
    dot_general x18 -> x2, matrix products: 17.8 us -> 1.92 us  [dot(): lax.dot_general(a, b, (((ca,), (cb,)), ((), ())), preferred_element_type=...]
    all_to_all x5 -> x4, waiting for transfers between devices: 53.6 us -> 42.6 us  [the longest x1 16.2 us: per_device(): lax.all_to_all(sent, SIDES, 0, 0, tiled=True)]
    all_to_all x5 -> x4, starting transfers between devices: 45.3 us -> 35.3 us  [the longest x1 13.5 us: per_device(): lax.all_to_all(sent, SIDES, 0, 0, tiled=True)]
    reshape x3 -> x0, other arithmetic: 2.85 us -> none  [the longest x2 1.91 us: dispatch(): sent.reshape(2 * experts, CAP, 2 * quarter)]
    ppermute x3, waiting for transfers between devices: 7.97 us -> 5.95 us  [the longest x1 5.95 us: per_device(): crossed_grad = lax.ppermute(hidden_grad, 'z_hi', SWAP)]
  transfers between devices with their start and end apart: 12 -> 11, of which waited for: 6 -> 5; matrix products, arithmetic and copies ran while one was open for 10% -> 5% of each run, Pallas kernels for 0% -> 7%
where the time goes in v3:
time: 157 us; the launch traced here: 156 us
  starting transfers between devices  55.7 us (35%)
  waiting for transfers between devices  48.6 us (31%)
  blocking collectives  26.2 us (17%)
  Pallas kernels  16.1 us (10%)
  other arithmetic  5.28 us (3%)
  matrix products  1.92 us (1%)
    all_gather x1, blocking collectives, per_device(): lax.all_gather(got[:, half:half + chunk].T, 'tensor', axis=0, tiled=True)  26.2 us
    all_to_all x1, waiting for transfers between devices, per_device(): lax.all_to_all(sent, SIDES, 0, 0, tiled=True)  16.2 us
    all_to_all x1, starting transfers between devices, per_device(): lax.all_to_all(sent, SIDES, 0, 0, tiled=True)  13.5 us
    all_to_all x1, waiting for transfers between devices, per_device(): lax.all_to_all(term.reshape(2 * experts, CAP, half), SIDES, 0, 0, tiled=T...  11 us
    all_to_all x1, starting transfers between devices, per_device(): lax.all_to_all(term.reshape(2 * experts, CAP, half), SIDES, 0, 0, tiled=T...  10.5 us
    all_to_all x1, waiting for transfers between devices, per_device(): both = lax.all_to_all(both, 'tensor', 0, 0, tiled=True)  8.14 us
    pallas_call x2, Pallas kernels, project(): pl.pallas_call(functools.partial(project_body, pairs, side), in_specs=[hb...  7.4 us
    all_to_all x1, waiting for transfers between devices, per_device(): mixed = lax.all_to_all(mixed, 'tensor', 0, 0, tiled=True)  7.31 us
  transfers between devices with their start and end apart: 11, of which 5 were waited for; matrix products, arithmetic and copies ran while one was open for 5% of the time, Pallas kernels for 7%

profile of v3, /device:TPU:2, one launch (start us, length us, event | category | flops | bytes accessed | tf_op | source)
XLA Modules:
  0.0 156.2 jit_solution(12955791188096523004)
XLA Ops:
  0.7 1.7 %shard_map.86 = bf16[8,24,640]{2,1,0:T(8,128)(2,1)} custom-call(bf16[24,384]{1,0:T(8,128)(2,1)} %x_rows.1, bf16[24,384]{1,0:T(8,128)(2,1)} %cotangent.1), custom_call_target="tpu_custom_call" | custom-call | bytes 600000 | tf_op jit(solution)/shard_map/pallas_call | solution.py:70
  2.3 7.1 %all-to-all-start = ((bf16[8,24,640]{2,1,0:T(8,128)(2,1)}), bf16[8,24,640]{2,1,0:T(8,128)(2,1)S(1)}, u32[]{:S(2)}, u32[]{:S(2)}) async-start(bf16[8,24,640]{2,1,0:T(8,128)(2,1)} %shard_map.86), calls=%async_computation | async-start | bytes 491520 | tf_op jit(solution)/shard_map/all_to_all | solution.py:278
  9.4 0.7 convert_reduce_fusion.2
  10.3 0.7 select_reduce_fusion.1
  11.0 0.7 multiply_add_fusion
  11.7 0.8 select_reduce_fusion
  12.8 8.1 %all-to-all-done.tokens = bf16[8,24,640]{2,1,0:T(8,128)(2,1)S(1)} async-done(((bf16[8,24,640]{2,1,0:T(8,128)(2,1)}), bf16[8,24,640]{2,1,0:T(8,128)(2,1)S(1)}, u32[]{:S(2)}, u32[]{:S(2)}) %all-to-all-start) | async-done | bytes 245792 | tf_op jit(solution)/shard_map/all_to_all | solution.py:278
  20.9 1.8 %shard_map.87 = bf16[2,128,1792]{2,1,0:T(8,128)(2,1)} custom-call(s32[2]{0:T(128)S(1)} %pad_add_fusion.place, bf16[8,24,640]{2,1,0:T(8,128)(2,1)S(1)} %all-to-all-done.tokens, bf16[128,24]{1,0:T(8,128)(2,1)S(1)} %copy.26.gather, f32[128,1]{1,0:T(8,128)S(1)} %copy.27.slot_weight), custom_call_target="tpu_custom_call" | custom-call | flops 18874368 | bytes 1600000 | tf_op jit(solution)/shard_map/pallas_call | solution.py:103
  22.7 13.5 %all-to-all-start.1 = ((bf16[32,8,1792]{2,1,0:T(8,128)(2,1)}), bf16[32,8,1792]{2,1,0:T(8,128)(2,1)S(1)}, u32[]{:S(2)}, u32[]{:S(2)}) async-start(bf16[32,8,1792]{2,1,0:T(8,128)(2,1)} %bitcast.46), calls=%async_computation.1 | async-start | bytes 1835008 | tf_op jit(solution)/shard_map/all_to_all | solution.py:288
  36.2 1.9 %collective-permute-start.2 = (bf16[672,768]{1,0:T(8,128)(2,1)S(1)}, bf16[672,768]{1,0:T(8,128)(2,1)S(1)}, u32[]{:S(2)}, u32[]{:S(2)}) collective-permute-start(bf16[672,768]{1,0:T(8,128)(2,1)S(1)} %bitcast.39), channel_id=1, source_target_pairs={{0,128},{128,0},{1,129},{129,1},{2,130},{130,2},{3,131},{131,3},{4... | collective-permute-start | bytes 3096584 | tf_op jit(solution)/shard_map/ppermute | solution.py:282
  38.1 2.4 %collective-permute-start.3 = (bf16[672,768]{1,0:T(8,128)(2,1)S(1)}, bf16[672,768]{1,0:T(8,128)(2,1)}, u32[]{:S(2)}, u32[]{:S(2)}) collective-permute-start(bf16[672,768]{1,0:T(8,128)(2,1)S(1)} %bitcast.42), channel_id=1, source_target_pairs={{0,128},{128,0},{1,129},{129,1},{2,130},{130,2},{3,131},{131,3},{4... | collective-permute-start | bytes 3096584 | tf_op jit(solution)/shard_map/ppermute | solution.py:283
  40.5 1.9 %collective-permute-start = (bf16[672,768]{1,0:T(8,128)(2,1)}, bf16[672,768]{1,0:T(8,128)(2,1)}, u32[]{:S(2)}, u32[]{:S(2)}) collective-permute-start(bf16[672,768]{1,0:T(8,128)(2,1)} %bitcast.48), channel_id=1, source_target_pairs={{0,128},{128,0},{1,129},{129,1},{2,130},{130,2},{3,131},{131,3},{4... | collective-permute-start | bytes 3096584 | tf_op jit(solution)/shard_map/ppermute | solution.py:284
  42.5 1.0 copy-done.3
  43.4 16.2 %all-to-all-done.1 = bf16[32,8,1792]{2,1,0:T(8,128)(2,1)S(1)} async-done(((bf16[32,8,1792]{2,1,0:T(8,128)(2,1)}), bf16[32,8,1792]{2,1,0:T(8,128)(2,1)S(1)}, u32[]{:S(2)}, u32[]{:S(2)}) %all-to-all-start.1) | async-done | bytes 917536 | tf_op jit(solution)/shard_map/all_to_all | solution.py:288
  59.6 4.0 %shard_map.89 = bf16[2,672,256]{2,1,0:T(8,128)(2,1)} custom-call(bf16[672,768]{1,0:T(8,128)(2,1)S(1)} %bitcast.40, bf16[672,768]{1,0:T(8,128)(2,1)S(1)} %bitcast.43, bf16[672,768]{1,0:T(8,128)(2,1)} %copy-done.3, bf16[672,768]{1,0:T(8,128)(2,1)} %collective-permute-done.3.refs_3_.refs_1_, bf16[256,1792]{1,0:T(8,128)(2,1)S(1)} %bitcast.37), custom_call_target="tpu_custom_call" | custom-call | flops 1056964608 | bytes 4128768 | tf_op jit(solution)/shard_map/pallas_call | solution.py:210
  63.6 3.4 %collective-permute-start.4 = (bf16[2,672,256]{2,1,0:T(8,128)(2,1)}, bf16[2,672,256]{2,1,0:T(8,128)(2,1)}, u32[]{:S(2)}, u32[]{:S(2)}) collective-permute-start(bf16[2,672,256]{2,1,0:T(8,128)(2,1)} %shard_map.89), channel_id=1, source_target_pairs={{0,256},{256,0},{1,257},{257,1},{2,258},{258,2},{3,259},{259,3},{4... | collective-permute-start | bytes 2064392 | tf_op jit(solution)/shard_map/ppermute | solution.py:292
  67.1 26.2 %all_gather.3.refs_2_ = bf16[1536,256]{1,0:T(8,128)(2,1)S(1)} all-gather(bf16[192,256]{1,0:T(8,128)(2,1)S(1)} %copy.28), channel_id=1, replica_groups=mesh['z_hi'=2,'core'=2,'z_lo'=4,'x'=4,'tensor'=8] {'tensor'}, dimensions={0}, use_global_device_ids=true | all-gather | bytes 884736 | tf_op jit(solution)/shard_map/all_gather | solution.py:293
  93.4 3.4 %shard_map.88.kept = bf16[1,672,256]{2,1,0:T(8,128)(2,1)} custom-call(bf16[672,768]{1,0:T(8,128)(2,1)} %bitcast.49, bf16[672,768]{1,0:T(8,128)(2,1)} %collective-permute-done.refs_1_, bf16[1536,256]{1,0:T(8,128)(2,1)S(1)} %all_gather.3.refs_2_), custom_call_target="tpu_custom_call" | custom-call | flops 528482304 | bytes 2064384 | tf_op jit(solution)/shard_map/pallas_call | solution.py:210
  96.8 6.5 %collective-permute-start.1 = (bf16[1,672,256]{2,1,0:T(8,128)(2,1)}, bf16[1,672,256]{2,1,0:T(8,128)(2,1)S(1)}, u32[]{:S(2)}, u32[]{:S(2)}) collective-permute-start(bf16[1,672,256]{2,1,0:T(8,128)(2,1)} %shard_map.88.kept), channel_id=1, source_target_pairs={{0,256},{256,0},{1,257},{257,1},{2,258},{258,2},{3,259},{259,3},{4... | collective-permute-start | bytes 1032200 | tf_op jit(solution)/shard_map/ppermute | solution.py:295
  103.3 1.2 convert_add_fusion
  104.5 1.7 %shard_map.90 = (bf16[672,768]{1,0:T(8,128)(2,1)S(1)}, bf16[672,768]{1,0:T(8,128)(2,1)S(1)}) custom-call(bf16[672,768]{1,0:T(8,128)(2,1)} %copy-done.3, bf16[672,768]{1,0:T(8,128)(2,1)} %collective-permute-done.3.refs_3_.refs_1_), custom_call_target="tpu_custom_call" | custom-call | bytes 4000000 | tf_op jit(solution)/shard_map/pallas_call | solution.py:150
  106.5 5.9 %collective-permute-done.1.crossed = bf16[1,672,256]{2,1,0:T(8,128)(2,1)S(1)} collective-permute-done((bf16[1,672,256]{2,1,0:T(8,128)(2,1)}, bf16[1,672,256]{2,1,0:T(8,128)(2,1)S(1)}, u32[]{:S(2)}, u32[]{:S(2)}) %collective-permute-start.1) | collective-permute-done | bytes 344096 | tf_op jit(solution)/shard_map/ppermute | solution.py:295
  112.5 2.2 %shard_map.91 = bf16[256,1536]{1,0:T(8,128)(2,1)} custom-call(bf16[1,672,256]{2,1,0:T(8,128)(2,1)S(1)} %copy-done.2, bf16[1,672,256]{2,1,0:T(8,128)(2,1)S(1)} %collective-permute-done.1.crossed, f32[672,256]{1,0:T(8,128)S(1)} %get-tuple-element.14.slope, f32[672,256]{1,0:T(8,128)S(1)} %get-tuple-element.13.active, bf16[672,768]{1,0:T(8,128)(2,1)S(1)} %bitcast.41, ...), custom_call_target="tpu_custom_call" | custom-call | flops 1056964608 | bytes 4128768 | tf_op jit(solution)/shard_map/pallas_call | solution.py:254
  114.7 10.5 %all-to-all-start.2 = ((bf16[32,8,1536]{2,1,0:T(8,128)(2,1)}), bf16[32,8,1536]{2,1,0:T(8,128)(2,1)S(1)}, u32[]{:S(2)}, u32[]{:S(2)}) async-start(bf16[32,8,1536]{2,1,0:T(8,128)(2,1)} %bitcast.47), calls=%async_computation.2 | async-start | bytes 1572864 | tf_op jit(solution)/shard_map/all_to_all | solution.py:311
  125.2 1.9 %collective-permute-start.6 = (bf16[768,256]{1,0:T(8,128)(2,1)S(1)}, bf16[768,256]{1,0:T(8,128)(2,1)S(1)}, u32[]{:S(2)}, u32[]{:S(2)}) collective-permute-start(bf16[768,256]{1,0:T(8,128)(2,1)S(1)} %slice.24), channel_id=1, source_target_pairs={{0,128},{128,0},{1,129},{129,1},{2,130},{130,2},{3,131},{131,3},{4... | collective-permute-start | bytes 1179656 | tf_op jit(solution)/shard_map/ppermute | solution.py:296
  127.1 2.4 %collective-permute-start.5 = (bf16[672,256]{1,0:T(8,128)(2,1)S(1)}, bf16[672,256]{1,0:T(8,128)(2,1)S(1)}, u32[]{:S(2)}, u32[]{:S(2)}) collective-permute-start(bf16[672,256]{1,0:T(8,128)(2,1)S(1)} %get-tuple-element.12), channel_id=1, source_target_pairs={{0,128},{128,0},{1,129},{129,1},{2,130},{130,2},{3,131},{131,3},{4... | collective-permute-start | bytes 1032200 | tf_op jit(solution)/shard_map/ppermute | solution.py:303
  129.6 11.0 %all-to-all-done.2 = bf16[32,8,1536]{2,1,0:T(8,128)(2,1)S(1)} async-done(((bf16[32,8,1536]{2,1,0:T(8,128)(2,1)}), bf16[32,8,1536]{2,1,0:T(8,128)(2,1)S(1)}, u32[]{:S(2)}, u32[]{:S(2)}) %all-to-all-start.2) | async-done | bytes 786464 | tf_op jit(solution)/shard_map/all_to_all | solution.py:311
  140.6 1.4 shard_map.92
  142.0 4.2 %all-to-all-start.3 = ((bf16[8,24,384]{2,1,0:T(8,128)(2,1)}), bf16[8,24,384]{2,1,0:T(8,128)(2,1)S(1)}, u32[]{:S(2)}, u32[]{:S(2)}) async-start(bf16[8,24,384]{2,1,0:T(8,128)(2,1)} %shard_map.92), calls=%async_computation.3 | async-start | bytes 294912 | tf_op jit(solution)/shard_map/all_to_all | solution.py:315
  146.8 1.5 fusion
  148.2 7.3 %all-to-all-done.3 = bf16[8,24,384]{2,1,0:T(8,128)(2,1)S(1)} async-done(((bf16[8,24,384]{2,1,0:T(8,128)(2,1)}), bf16[8,24,384]{2,1,0:T(8,128)(2,1)S(1)}, u32[]{:S(2)}, u32[]{:S(2)}) %all-to-all-start.3) | async-done | bytes 147488 | tf_op jit(solution)/shard_map/all_to_all | solution.py:315
  155.5 0.6 reduce_sum.62
  (28 shorter events, 1.6 us)
Async XLA Ops:
  0.6 35.5 %copy-start = (bf16[1,768,672]{1,2,0:T(8,128)(2,1)S(1)}, bf16[1,768,672]{1,2,0:T(8,128)(2,1)}, u32[]{:S(2)}) copy-start(bf16[1,768,672]{1,2,0:T(8,128)(2,1)} %param.11) | copy-start | bytes 3096580
  0.6 37.5 %copy-start.1 = (bf16[1,768,672]{1,2,0:T(8,128)(2,1)S(1)}, bf16[1,768,672]{1,2,0:T(8,128)(2,1)}, u32[]{:S(2)}) copy-start(bf16[1,768,672]{1,2,0:T(8,128)(2,1)} %param.12) | copy-start | bytes 3096580
  2.3 18.6 %all-to-all-start = ((bf16[8,24,640]{2,1,0:T(8,128)(2,1)}), bf16[8,24,640]{2,1,0:T(8,128)(2,1)S(1)}, u32[]{:S(2)}, u32[]{:S(2)}) async-start(bf16[8,24,640]{2,1,0:T(8,128)(2,1)} %shard_map.86), calls=%async_computation | async-start | bytes 491520 | tf_op jit(solution)/shard_map/all_to_all | solution.py:278
  22.7 36.9 %all-to-all-start.1 = ((bf16[32,8,1792]{2,1,0:T(8,128)(2,1)}), bf16[32,8,1792]{2,1,0:T(8,128)(2,1)S(1)}, u32[]{:S(2)}, u32[]{:S(2)}) async-start(bf16[32,8,1792]{2,1,0:T(8,128)(2,1)} %bitcast.46), calls=%async_computation.1 | async-start | bytes 1835008 | tf_op jit(solution)/shard_map/all_to_all | solution.py:288
  36.2 6.3 %collective-permute-start.2 = (bf16[672,768]{1,0:T(8,128)(2,1)S(1)}, bf16[672,768]{1,0:T(8,128)(2,1)S(1)}, u32[]{:S(2)}, u32[]{:S(2)}) collective-permute-start(bf16[672,768]{1,0:T(8,128)(2,1)S(1)} %bitcast.39), channel_id=1, source_target_pairs={{0,128},{128,0},{1,129},{129,1},{2,130},{130,2},{3,131},{131,3},{4... | collective-permute-start | bytes 3096584 | tf_op jit(solution)/shard_map/ppermute | solution.py:282
  38.1 5.3 %collective-permute-start.3 = (bf16[672,768]{1,0:T(8,128)(2,1)S(1)}, bf16[672,768]{1,0:T(8,128)(2,1)}, u32[]{:S(2)}, u32[]{:S(2)}) collective-permute-start(bf16[672,768]{1,0:T(8,128)(2,1)S(1)} %bitcast.42), channel_id=1, source_target_pairs={{0,128},{128,0},{1,129},{129,1},{2,130},{130,2},{3,131},{131,3},{4... | collective-permute-start | bytes 3096584 | tf_op jit(solution)/shard_map/ppermute | solution.py:283
  40.5 52.8 %collective-permute-start = (bf16[672,768]{1,0:T(8,128)(2,1)}, bf16[672,768]{1,0:T(8,128)(2,1)}, u32[]{:S(2)}, u32[]{:S(2)}) collective-permute-start(bf16[672,768]{1,0:T(8,128)(2,1)} %bitcast.48), channel_id=1, source_target_pairs={{0,128},{128,0},{1,129},{129,1},{2,130},{130,2},{3,131},{131,3},{4... | collective-permute-start | bytes 3096584 | tf_op jit(solution)/shard_map/ppermute | solution.py:284
  42.5 1.0 copy-start.3
  63.6 39.7 %collective-permute-start.4 = (bf16[2,672,256]{2,1,0:T(8,128)(2,1)}, bf16[2,672,256]{2,1,0:T(8,128)(2,1)}, u32[]{:S(2)}, u32[]{:S(2)}) collective-permute-start(bf16[2,672,256]{2,1,0:T(8,128)(2,1)} %shard_map.89), channel_id=1, source_target_pairs={{0,256},{256,0},{1,257},{257,1},{2,258},{258,2},{3,259},{259,3},{4... | collective-permute-start | bytes 2064392 | tf_op jit(solution)/shard_map/ppermute | solution.py:292
  67.1 36.2 %copy-start.4 = (bf16[2,672,256]{2,1,0:T(8,128)(2,1)S(1)}, bf16[2,672,256]{2,1,0:T(8,128)(2,1)}, u32[]{:S(2)}) copy-start(bf16[2,672,256]{2,1,0:T(8,128)(2,1)} %shard_map.89) | copy-start | bytes 2064388
  96.8 15.7 %collective-permute-start.1 = (bf16[1,672,256]{2,1,0:T(8,128)(2,1)}, bf16[1,672,256]{2,1,0:T(8,128)(2,1)S(1)}, u32[]{:S(2)}, u32[]{:S(2)}) collective-permute-start(bf16[1,672,256]{2,1,0:T(8,128)(2,1)} %shard_map.88.kept), channel_id=1, source_target_pairs={{0,256},{256,0},{1,257},{257,1},{2,258},{258,2},{3,259},{259,3},{4... | collective-permute-start | bytes 1032200 | tf_op jit(solution)/shard_map/ppermute | solution.py:295
  106.2 6.3 %copy-start.2 = (bf16[1,672,256]{2,1,0:T(8,128)(2,1)S(1)}, bf16[1,672,256]{2,1,0:T(8,128)(2,1)}, u32[]{:S(2)}) copy-start(bf16[1,672,256]{2,1,0:T(8,128)(2,1)} %shard_map.88.kept) | copy-start | bytes 1032196
  114.7 25.9 %all-to-all-start.2 = ((bf16[32,8,1536]{2,1,0:T(8,128)(2,1)}), bf16[32,8,1536]{2,1,0:T(8,128)(2,1)S(1)}, u32[]{:S(2)}, u32[]{:S(2)}) async-start(bf16[32,8,1536]{2,1,0:T(8,128)(2,1)} %bitcast.47), calls=%async_computation.2 | async-start | bytes 1572864 | tf_op jit(solution)/shard_map/all_to_all | solution.py:311
  125.2 21.6 %collective-permute-start.6 = (bf16[768,256]{1,0:T(8,128)(2,1)S(1)}, bf16[768,256]{1,0:T(8,128)(2,1)S(1)}, u32[]{:S(2)}, u32[]{:S(2)}) collective-permute-start(bf16[768,256]{1,0:T(8,128)(2,1)S(1)} %slice.24), channel_id=1, source_target_pairs={{0,128},{128,0},{1,129},{129,1},{2,130},{130,2},{3,131},{131,3},{4... | collective-permute-start | bytes 1179656 | tf_op jit(solution)/shard_map/ppermute | solution.py:296
  127.1 19.6 %collective-permute-start.5 = (bf16[672,256]{1,0:T(8,128)(2,1)S(1)}, bf16[672,256]{1,0:T(8,128)(2,1)S(1)}, u32[]{:S(2)}, u32[]{:S(2)}) collective-permute-start(bf16[672,256]{1,0:T(8,128)(2,1)S(1)} %get-tuple-element.12), channel_id=1, source_target_pairs={{0,128},{128,0},{1,129},{129,1},{2,130},{130,2},{3,131},{131,3},{4... | collective-permute-start | bytes 1032200 | tf_op jit(solution)/shard_map/ppermute | solution.py:303
  142.0 13.5 %all-to-all-start.3 = ((bf16[8,24,384]{2,1,0:T(8,128)(2,1)}), bf16[8,24,384]{2,1,0:T(8,128)(2,1)S(1)}, u32[]{:S(2)}, u32[]{:S(2)}) async-start(bf16[8,24,384]{2,1,0:T(8,128)(2,1)} %shard_map.92), calls=%async_computation.3 | async-start | bytes 294912 | tf_op jit(solution)/shard_map/all_to_all | solution.py:315

commit v4 on v3

--- a/solution.py
+++ b/solution.py
@@ -81,17 +81,25 @@
     core, turn = place[0], place[1]
     piece = tokens.shape[2] - 256
     stores = []
+
+    def leaves(z, i, where):
+        stores.append(
+            pltpu.make_async_copy(held.at[z, :, where], out.at[z, :, where], leave.at[z, i])
+        )
+        stores[-1].start()
+
     for z in range(2):
         for k in range(4):
             which = z * 4 + (core * 2 if k < 2 else 2 - core * 2) + k % 2
             part = dot(gather[...], tokens[which, :, :piece], 1, 0)
             held[z, :, k * piece : (k + 1) * piece] = part.astype(BF16)
+            if k % 2 == 1:
+                leaves(z, k // 2, pl.ds((k - 1) * piece, 2 * piece))
         k = turn // 2
         which = z * 4 + jnp.where(k < 2, core * 2, 2 - core * 2) + k % 2
         dy = dot(gather[...], tokens[which, :, piece:], 1, 0) * slot_weight[...]
         held[z, :, 4 * piece :] = dy.astype(BF16)
-        stores.append(pltpu.make_async_copy(held.at[z], out.at[z], leave.at[z]))
-        stores[-1].start()
+        leaves(z, 2, pl.ds(4 * piece, 256))
     for store in stores:
         store.wait()
 
@@ -105,20 +113,27 @@
         in_specs=[pl.BlockSpec(memory_space=pltpu.SMEM), vmem, vmem, vmem],
         out_specs=pl.BlockSpec(memory_space=pl.ANY),
         out_shape=pltpu.HBM(shape, BF16),
-        scratch_shapes=[pltpu.VMEM(shape, BF16), pltpu.SemaphoreType.DMA((2,))],
+        scratch_shapes=[pltpu.VMEM(shape, BF16), pltpu.SemaphoreType.DMA((2, 3))],
         compiler_params=params(),
         cost_estimate=cost(2 * 24 * 8 * 384 * 128, 1600000),
     )(place, tokens, gather, slot_weight)
 
 
-def combine_body(place, returned, select, out):
+def combine_body(place, returned, select, out, held, leave):
     core = place[0]
     piece = out.shape[2]
+    stores = []
     for z in range(2):
+        mixed = dot(select[...], returned[z], 1, 0).astype(BF16)
         for k in range(4):
             which = z * 4 + (core * 2 if k < 2 else 2 - core * 2) + k % 2
-            part = returned[z, :, k * piece : (k + 1) * piece]
-            out[which] = dot(select[...], part, 1, 0).astype(BF16)
+            held[z * 4 + k] = mixed[:, k * piece : (k + 1) * piece]
+            stores.append(
+                pltpu.make_async_copy(held.at[z * 4 + k], out.at[which], leave.at[z, k])
+            )
+            stores[-1].start()
+    for store in stores:
+        store.wait()
 
 
 def combine(place, returned, select, tensor):
@@ -127,8 +142,12 @@
     return pl.pallas_call(
         combine_body,
         in_specs=[pl.BlockSpec(memory_space=pltpu.SMEM), vmem, vmem],
-        out_specs=vmem,
-        out_shape=jax.ShapeDtypeStruct((tensor, tokens, 2 * returned.shape[2] // tensor), BF16),
+        out_specs=pl.BlockSpec(memory_space=pl.ANY),
+        out_shape=pltpu.HBM((tensor, tokens, 2 * returned.shape[2] // tensor), BF16),
+        scratch_shapes=[
+            pltpu.VMEM((tensor, tokens, 2 * returned.shape[2] // tensor), BF16),
+            pltpu.SemaphoreType.DMA((2, 4)),
+        ],
         compiler_params=params(),
         cost_estimate=cost(2 * 24 * 128 * 3072, 1000000),
     )(place, returned, select)
@@ -204,7 +223,7 @@
 def project(own, far, act, side, count, fetch_own):
     pairs = len(own)
     hidden, quarter = own[0].shape
-    parts = 3
+    parts = 2
     vmem, hbm = pl.BlockSpec(memory_space=pltpu.VMEM), pl.BlockSpec(memory_space=pl.ANY)
     fetched = 2 * pairs if fetch_own else pairs
     return pl.pallas_call(

time: 157 us -> 156 us (level)
  transfers between devices with their start and end apart: 11 -> 11, of which waited for: 5 -> 5; matrix products, arithmetic and copies ran while one was open for 5% -> 5% of each run, Pallas kernels for 7% -> 6%
where the time goes in v4:
time: 156 us
  starting transfers between devices  55.6 us (36%)
  waiting for transfers between devices  48.7 us (31%)
  blocking collectives  26.2 us (17%)
  Pallas kernels  15.5 us (10%)
  other arithmetic  5.28 us (3%)
  matrix products  1.9 us (1%)
    all_gather x1, blocking collectives, per_device(): lax.all_gather(got[:, half:half + chunk].T, 'tensor', axis=0, tiled=True)  26.2 us
    all_to_all x1, waiting for transfers between devices, per_device(): lax.all_to_all(sent, SIDES, 0, 0, tiled=True)  16.2 us
    all_to_all x1, starting transfers between devices, per_device(): lax.all_to_all(sent, SIDES, 0, 0, tiled=True)  13.5 us
    all_to_all x1, waiting for transfers between devices, per_device(): lax.all_to_all(term.reshape(2 * experts, CAP, half), SIDES, 0, 0, tiled=T...  11 us
    all_to_all x1, starting transfers between devices, per_device(): lax.all_to_all(term.reshape(2 * experts, CAP, half), SIDES, 0, 0, tiled=T...  10.6 us
    all_to_all x1, waiting for transfers between devices, per_device(): both = lax.all_to_all(both, 'tensor', 0, 0, tiled=True)  8.14 us
    all_to_all x1, waiting for transfers between devices, per_device(): mixed = lax.all_to_all(mixed, 'tensor', 0, 0, tiled=True)  7.33 us
    all_to_all x1, starting transfers between devices, per_device(): both = lax.all_to_all(both, 'tensor', 0, 0, tiled=True)  7.1 us
  transfers between devices with their start and end apart: 11, of which 5 were waited for; matrix products, arithmetic and copies ran while one was open for 5% of the time, Pallas kernels for 6%

profile of v4, /device:TPU:2, one launch (start us, length us, event | category | flops | bytes accessed | tf_op | source)
XLA Modules:
  0.0 155.5 jit_solution(16912935417552736235)
XLA Ops:
  0.7 1.7 %shard_map.86 = bf16[8,24,640]{2,1,0:T(8,128)(2,1)} custom-call(bf16[24,384]{1,0:T(8,128)(2,1)} %x_rows.1, bf16[24,384]{1,0:T(8,128)(2,1)} %cotangent.1), custom_call_target="tpu_custom_call" | custom-call | bytes 600000 | tf_op jit(solution)/shard_map/pallas_call | solution.py:70
  2.3 7.1 %all-to-all-start = ((bf16[8,24,640]{2,1,0:T(8,128)(2,1)}), bf16[8,24,640]{2,1,0:T(8,128)(2,1)S(1)}, u32[]{:S(2)}, u32[]{:S(2)}) async-start(bf16[8,24,640]{2,1,0:T(8,128)(2,1)} %shard_map.86), calls=%async_computation | async-start | bytes 491520 | tf_op jit(solution)/shard_map/all_to_all | solution.py:297
  9.4 0.7 convert_reduce_fusion.2
  10.3 0.7 select_reduce_fusion.1
  11.0 0.7 multiply_add_fusion
  11.7 0.8 select_reduce_fusion
  12.8 8.1 %all-to-all-done.tokens = bf16[8,24,640]{2,1,0:T(8,128)(2,1)S(1)} async-done(((bf16[8,24,640]{2,1,0:T(8,128)(2,1)}), bf16[8,24,640]{2,1,0:T(8,128)(2,1)S(1)}, u32[]{:S(2)}, u32[]{:S(2)}) %all-to-all-start) | async-done | bytes 245792 | tf_op jit(solution)/shard_map/all_to_all | solution.py:297
  20.9 1.8 %shard_map.87 = bf16[2,128,1792]{2,1,0:T(8,128)(2,1)} custom-call(s32[2]{0:T(128)S(1)} %pad_add_fusion.place, bf16[8,24,640]{2,1,0:T(8,128)(2,1)S(1)} %all-to-all-done.tokens, bf16[128,24]{1,0:T(8,128)(2,1)S(1)} %copy.26.gather, f32[128,1]{1,0:T(8,128)S(1)} %copy.27.slot_weight), custom_call_target="tpu_custom_call" | custom-call | flops 18874368 | bytes 1600000 | tf_op jit(solution)/shard_map/pallas_call | solution.py:111
  22.7 13.5 %all-to-all-start.1 = ((bf16[32,8,1792]{2,1,0:T(8,128)(2,1)}), bf16[32,8,1792]{2,1,0:T(8,128)(2,1)S(1)}, u32[]{:S(2)}, u32[]{:S(2)}) async-start(bf16[32,8,1792]{2,1,0:T(8,128)(2,1)} %bitcast.46), calls=%async_computation.1 | async-start | bytes 1835008 | tf_op jit(solution)/shard_map/all_to_all | solution.py:307
  36.2 1.9 %collective-permute-start.2 = (bf16[672,768]{1,0:T(8,128)(2,1)S(1)}, bf16[672,768]{1,0:T(8,128)(2,1)S(1)}, u32[]{:S(2)}, u32[]{:S(2)}) collective-permute-start(bf16[672,768]{1,0:T(8,128)(2,1)S(1)} %bitcast.39), channel_id=1, source_target_pairs={{0,128},{128,0},{1,129},{129,1},{2,130},{130,2},{3,131},{131,3},{4... | collective-permute-start | bytes 3096584 | tf_op jit(solution)/shard_map/ppermute | solution.py:301
  38.1 2.4 %collective-permute-start.3 = (bf16[672,768]{1,0:T(8,128)(2,1)S(1)}, bf16[672,768]{1,0:T(8,128)(2,1)}, u32[]{:S(2)}, u32[]{:S(2)}) collective-permute-start(bf16[672,768]{1,0:T(8,128)(2,1)S(1)} %bitcast.42), channel_id=1, source_target_pairs={{0,128},{128,0},{1,129},{129,1},{2,130},{130,2},{3,131},{131,3},{4... | collective-permute-start | bytes 3096584 | tf_op jit(solution)/shard_map/ppermute | solution.py:302
  40.5 1.9 %collective-permute-start = (bf16[672,768]{1,0:T(8,128)(2,1)}, bf16[672,768]{1,0:T(8,128)(2,1)}, u32[]{:S(2)}, u32[]{:S(2)}) collective-permute-start(bf16[672,768]{1,0:T(8,128)(2,1)} %bitcast.48), channel_id=1, source_target_pairs={{0,128},{128,0},{1,129},{129,1},{2,130},{130,2},{3,131},{131,3},{4... | collective-permute-start | bytes 3096584 | tf_op jit(solution)/shard_map/ppermute | solution.py:303
  42.5 1.0 copy-done.3
  43.4 16.2 %all-to-all-done.1 = bf16[32,8,1792]{2,1,0:T(8,128)(2,1)S(1)} async-done(((bf16[32,8,1792]{2,1,0:T(8,128)(2,1)}), bf16[32,8,1792]{2,1,0:T(8,128)(2,1)S(1)}, u32[]{:S(2)}, u32[]{:S(2)}) %all-to-all-start.1) | async-done | bytes 917536 | tf_op jit(solution)/shard_map/all_to_all | solution.py:307
  59.6 3.6 %shard_map.89 = bf16[2,672,256]{2,1,0:T(8,128)(2,1)} custom-call(bf16[672,768]{1,0:T(8,128)(2,1)S(1)} %bitcast.40, bf16[672,768]{1,0:T(8,128)(2,1)S(1)} %bitcast.43, bf16[672,768]{1,0:T(8,128)(2,1)} %copy-done.3, bf16[672,768]{1,0:T(8,128)(2,1)} %collective-permute-done.3.refs_3_.refs_1_, bf16[256,1792]{1,0:T(8,128)(2,1)S(1)} %bitcast.37), custom_call_target="tpu_custom_call" | custom-call | flops 1056964608 | bytes 4128768 | tf_op jit(solution)/shard_map/pallas_call | solution.py:229
  63.2 3.4 %collective-permute-start.4 = (bf16[2,672,256]{2,1,0:T(8,128)(2,1)}, bf16[2,672,256]{2,1,0:T(8,128)(2,1)}, u32[]{:S(2)}, u32[]{:S(2)}) collective-permute-start(bf16[2,672,256]{2,1,0:T(8,128)(2,1)} %shard_map.89), channel_id=1, source_target_pairs={{0,256},{256,0},{1,257},{257,1},{2,258},{258,2},{3,259},{259,3},{4... | collective-permute-start | bytes 2064392 | tf_op jit(solution)/shard_map/ppermute | solution.py:311
  66.7 26.2 %all_gather.3.refs_2_ = bf16[1536,256]{1,0:T(8,128)(2,1)S(1)} all-gather(bf16[192,256]{1,0:T(8,128)(2,1)S(1)} %copy.28), channel_id=1, replica_groups=mesh['z_hi'=2,'core'=2,'z_lo'=4,'x'=4,'tensor'=8] {'tensor'}, dimensions={0}, use_global_device_ids=true | all-gather | bytes 884736 | tf_op jit(solution)/shard_map/all_gather | solution.py:312
  92.9 3.2 %shard_map.88.kept = bf16[1,672,256]{2,1,0:T(8,128)(2,1)} custom-call(bf16[672,768]{1,0:T(8,128)(2,1)} %bitcast.49, bf16[672,768]{1,0:T(8,128)(2,1)} %collective-permute-done.refs_1_, bf16[1536,256]{1,0:T(8,128)(2,1)S(1)} %all_gather.3.refs_2_), custom_call_target="tpu_custom_call" | custom-call | flops 528482304 | bytes 2064384 | tf_op jit(solution)/shard_map/pallas_call | solution.py:229
  96.1 6.5 %collective-permute-start.1 = (bf16[1,672,256]{2,1,0:T(8,128)(2,1)}, bf16[1,672,256]{2,1,0:T(8,128)(2,1)S(1)}, u32[]{:S(2)}, u32[]{:S(2)}) collective-permute-start(bf16[1,672,256]{2,1,0:T(8,128)(2,1)} %shard_map.88.kept), channel_id=1, source_target_pairs={{0,256},{256,0},{1,257},{257,1},{2,258},{258,2},{3,259},{259,3},{4... | collective-permute-start | bytes 1032200 | tf_op jit(solution)/shard_map/ppermute | solution.py:314
  102.6 1.2 convert_add_fusion
  103.9 1.7 %shard_map.90 = (bf16[672,768]{1,0:T(8,128)(2,1)S(1)}, bf16[672,768]{1,0:T(8,128)(2,1)S(1)}) custom-call(bf16[672,768]{1,0:T(8,128)(2,1)} %copy-done.3, bf16[672,768]{1,0:T(8,128)(2,1)} %collective-permute-done.3.refs_3_.refs_1_), custom_call_target="tpu_custom_call" | custom-call | bytes 4000000 | tf_op jit(solution)/shard_map/pallas_call | solution.py:169
  105.9 6.1 %collective-permute-done.1.crossed = bf16[1,672,256]{2,1,0:T(8,128)(2,1)S(1)} collective-permute-done((bf16[1,672,256]{2,1,0:T(8,128)(2,1)}, bf16[1,672,256]{2,1,0:T(8,128)(2,1)S(1)}, u32[]{:S(2)}, u32[]{:S(2)}) %collective-permute-start.1) | collective-permute-done | bytes 344096 | tf_op jit(solution)/shard_map/ppermute | solution.py:314
  112.0 2.2 %shard_map.91 = bf16[256,1536]{1,0:T(8,128)(2,1)} custom-call(bf16[1,672,256]{2,1,0:T(8,128)(2,1)S(1)} %copy-done.2, bf16[1,672,256]{2,1,0:T(8,128)(2,1)S(1)} %collective-permute-done.1.crossed, f32[672,256]{1,0:T(8,128)S(1)} %get-tuple-element.14.slope, f32[672,256]{1,0:T(8,128)S(1)} %get-tuple-element.13.active, bf16[672,768]{1,0:T(8,128)(2,1)S(1)} %bitcast.41, ...), custom_call_target="tpu_custom_call" | custom-call | flops 1056964608 | bytes 4128768 | tf_op jit(solution)/shard_map/pallas_call | solution.py:273
  114.2 10.6 %all-to-all-start.2 = ((bf16[32,8,1536]{2,1,0:T(8,128)(2,1)}), bf16[32,8,1536]{2,1,0:T(8,128)(2,1)S(1)}, u32[]{:S(2)}, u32[]{:S(2)}) async-start(bf16[32,8,1536]{2,1,0:T(8,128)(2,1)} %bitcast.47), calls=%async_computation.2 | async-start | bytes 1572864 | tf_op jit(solution)/shard_map/all_to_all | solution.py:330
  124.8 1.9 %collective-permute-start.6 = (bf16[768,256]{1,0:T(8,128)(2,1)S(1)}, bf16[768,256]{1,0:T(8,128)(2,1)S(1)}, u32[]{:S(2)}, u32[]{:S(2)}) collective-permute-start(bf16[768,256]{1,0:T(8,128)(2,1)S(1)} %slice.24), channel_id=1, source_target_pairs={{0,128},{128,0},{1,129},{129,1},{2,130},{130,2},{3,131},{131,3},{4... | collective-permute-start | bytes 1179656 | tf_op jit(solution)/shard_map/ppermute | solution.py:315
  126.7 2.4 %collective-permute-start.5 = (bf16[672,256]{1,0:T(8,128)(2,1)S(1)}, bf16[672,256]{1,0:T(8,128)(2,1)S(1)}, u32[]{:S(2)}, u32[]{:S(2)}) collective-permute-start(bf16[672,256]{1,0:T(8,128)(2,1)S(1)} %get-tuple-element.12), channel_id=1, source_target_pairs={{0,128},{128,0},{1,129},{129,1},{2,130},{130,2},{3,131},{131,3},{4... | collective-permute-start | bytes 1032200 | tf_op jit(solution)/shard_map/ppermute | solution.py:322
  129.2 11.0 %all-to-all-done.2 = bf16[32,8,1536]{2,1,0:T(8,128)(2,1)S(1)} async-done(((bf16[32,8,1536]{2,1,0:T(8,128)(2,1)}), bf16[32,8,1536]{2,1,0:T(8,128)(2,1)S(1)}, u32[]{:S(2)}, u32[]{:S(2)}) %all-to-all-start.2) | async-done | bytes 786464 | tf_op jit(solution)/shard_map/all_to_all | solution.py:330
  140.2 1.5 shard_map.92
  141.6 4.0 %all-to-all-start.3 = ((bf16[8,24,384]{2,1,0:T(8,128)(2,1)}), bf16[8,24,384]{2,1,0:T(8,128)(2,1)S(1)}, u32[]{:S(2)}, u32[]{:S(2)}) async-start(bf16[8,24,384]{2,1,0:T(8,128)(2,1)} %shard_map.92), calls=%async_computation.3 | async-start | bytes 294912 | tf_op jit(solution)/shard_map/all_to_all | solution.py:334
  146.1 1.4 fusion
  147.6 7.3 %all-to-all-done.3 = bf16[8,24,384]{2,1,0:T(8,128)(2,1)S(1)} async-done(((bf16[8,24,384]{2,1,0:T(8,128)(2,1)}), bf16[8,24,384]{2,1,0:T(8,128)(2,1)S(1)}, u32[]{:S(2)}, u32[]{:S(2)}) %all-to-all-start.3) | async-done | bytes 147488 | tf_op jit(solution)/shard_map/all_to_all | solution.py:334
  154.9 0.6 reduce_sum.62
  (28 shorter events, 1.6 us)
Async XLA Ops:
  0.6 35.5 %copy-start = (bf16[1,768,672]{1,2,0:T(8,128)(2,1)S(1)}, bf16[1,768,672]{1,2,0:T(8,128)(2,1)}, u32[]{:S(2)}) copy-start(bf16[1,768,672]{1,2,0:T(8,128)(2,1)} %param.11) | copy-start | bytes 3096580
  0.6 37.5 %copy-start.1 = (bf16[1,768,672]{1,2,0:T(8,128)(2,1)S(1)}, bf16[1,768,672]{1,2,0:T(8,128)(2,1)}, u32[]{:S(2)}) copy-start(bf16[1,768,672]{1,2,0:T(8,128)(2,1)} %param.12) | copy-start | bytes 3096580
  2.3 18.6 %all-to-all-start = ((bf16[8,24,640]{2,1,0:T(8,128)(2,1)}), bf16[8,24,640]{2,1,0:T(8,128)(2,1)S(1)}, u32[]{:S(2)}, u32[]{:S(2)}) async-start(bf16[8,24,640]{2,1,0:T(8,128)(2,1)} %shard_map.86), calls=%async_computation | async-start | bytes 491520 | tf_op jit(solution)/shard_map/all_to_all | solution.py:297
  22.7 36.9 %all-to-all-start.1 = ((bf16[32,8,1792]{2,1,0:T(8,128)(2,1)}), bf16[32,8,1792]{2,1,0:T(8,128)(2,1)S(1)}, u32[]{:S(2)}, u32[]{:S(2)}) async-start(bf16[32,8,1792]{2,1,0:T(8,128)(2,1)} %bitcast.46), calls=%async_computation.1 | async-start | bytes 1835008 | tf_op jit(solution)/shard_map/all_to_all | solution.py:307
  36.2 6.3 %collective-permute-start.2 = (bf16[672,768]{1,0:T(8,128)(2,1)S(1)}, bf16[672,768]{1,0:T(8,128)(2,1)S(1)}, u32[]{:S(2)}, u32[]{:S(2)}) collective-permute-start(bf16[672,768]{1,0:T(8,128)(2,1)S(1)} %bitcast.39), channel_id=1, source_target_pairs={{0,128},{128,0},{1,129},{129,1},{2,130},{130,2},{3,131},{131,3},{4... | collective-permute-start | bytes 3096584 | tf_op jit(solution)/shard_map/ppermute | solution.py:301
  38.1 5.3 %collective-permute-start.3 = (bf16[672,768]{1,0:T(8,128)(2,1)S(1)}, bf16[672,768]{1,0:T(8,128)(2,1)}, u32[]{:S(2)}, u32[]{:S(2)}) collective-permute-start(bf16[672,768]{1,0:T(8,128)(2,1)S(1)} %bitcast.42), channel_id=1, source_target_pairs={{0,128},{128,0},{1,129},{129,1},{2,130},{130,2},{3,131},{131,3},{4... | collective-permute-start | bytes 3096584 | tf_op jit(solution)/shard_map/ppermute | solution.py:302
  40.5 52.4 %collective-permute-start = (bf16[672,768]{1,0:T(8,128)(2,1)}, bf16[672,768]{1,0:T(8,128)(2,1)}, u32[]{:S(2)}, u32[]{:S(2)}) collective-permute-start(bf16[672,768]{1,0:T(8,128)(2,1)} %bitcast.48), channel_id=1, source_target_pairs={{0,128},{128,0},{1,129},{129,1},{2,130},{130,2},{3,131},{131,3},{4... | collective-permute-start | bytes 3096584 | tf_op jit(solution)/shard_map/ppermute | solution.py:303
  42.5 1.0 copy-start.3
  63.2 39.4 %collective-permute-start.4 = (bf16[2,672,256]{2,1,0:T(8,128)(2,1)}, bf16[2,672,256]{2,1,0:T(8,128)(2,1)}, u32[]{:S(2)}, u32[]{:S(2)}) collective-permute-start(bf16[2,672,256]{2,1,0:T(8,128)(2,1)} %shard_map.89), channel_id=1, source_target_pairs={{0,256},{256,0},{1,257},{257,1},{2,258},{258,2},{3,259},{259,3},{4... | collective-permute-start | bytes 2064392 | tf_op jit(solution)/shard_map/ppermute | solution.py:311
  66.7 35.9 %copy-start.4 = (bf16[2,672,256]{2,1,0:T(8,128)(2,1)S(1)}, bf16[2,672,256]{2,1,0:T(8,128)(2,1)}, u32[]{:S(2)}) copy-start(bf16[2,672,256]{2,1,0:T(8,128)(2,1)} %shard_map.89) | copy-start | bytes 2064388
  96.1 15.9 %collective-permute-start.1 = (bf16[1,672,256]{2,1,0:T(8,128)(2,1)}, bf16[1,672,256]{2,1,0:T(8,128)(2,1)S(1)}, u32[]{:S(2)}, u32[]{:S(2)}) collective-permute-start(bf16[1,672,256]{2,1,0:T(8,128)(2,1)} %shard_map.88.kept), channel_id=1, source_target_pairs={{0,256},{256,0},{1,257},{257,1},{2,258},{258,2},{3,259},{259,3},{4... | collective-permute-start | bytes 1032200 | tf_op jit(solution)/shard_map/ppermute | solution.py:314
  105.5 6.4 %copy-start.2 = (bf16[1,672,256]{2,1,0:T(8,128)(2,1)S(1)}, bf16[1,672,256]{2,1,0:T(8,128)(2,1)}, u32[]{:S(2)}) copy-start(bf16[1,672,256]{2,1,0:T(8,128)(2,1)} %shard_map.88.kept) | copy-start | bytes 1032196
  114.2 26.0 %all-to-all-start.2 = ((bf16[32,8,1536]{2,1,0:T(8,128)(2,1)}), bf16[32,8,1536]{2,1,0:T(8,128)(2,1)S(1)}, u32[]{:S(2)}, u32[]{:S(2)}) async-start(bf16[32,8,1536]{2,1,0:T(8,128)(2,1)} %bitcast.47), calls=%async_computation.2 | async-start | bytes 1572864 | tf_op jit(solution)/shard_map/all_to_all | solution.py:330
  124.8 21.3 %collective-permute-start.6 = (bf16[768,256]{1,0:T(8,128)(2,1)S(1)}, bf16[768,256]{1,0:T(8,128)(2,1)S(1)}, u32[]{:S(2)}, u32[]{:S(2)}) collective-permute-start(bf16[768,256]{1,0:T(8,128)(2,1)S(1)} %slice.24), channel_id=1, source_target_pairs={{0,128},{128,0},{1,129},{129,1},{2,130},{130,2},{3,131},{131,3},{4... | collective-permute-start | bytes 1179656 | tf_op jit(solution)/shard_map/ppermute | solution.py:315
  126.7 19.4 %collective-permute-start.5 = (bf16[672,256]{1,0:T(8,128)(2,1)S(1)}, bf16[672,256]{1,0:T(8,128)(2,1)S(1)}, u32[]{:S(2)}, u32[]{:S(2)}) collective-permute-start(bf16[672,256]{1,0:T(8,128)(2,1)S(1)} %get-tuple-element.12), channel_id=1, source_target_pairs={{0,128},{128,0},{1,129},{129,1},{2,130},{130,2},{3,131},{131,3},{4... | collective-permute-start | bytes 1032200 | tf_op jit(solution)/shard_map/ppermute | solution.py:322
  141.6 13.3 %all-to-all-start.3 = ((bf16[8,24,384]{2,1,0:T(8,128)(2,1)}), bf16[8,24,384]{2,1,0:T(8,128)(2,1)S(1)}, u32[]{:S(2)}, u32[]{:S(2)}) async-start(bf16[8,24,384]{2,1,0:T(8,128)(2,1)} %shard_map.92), calls=%async_computation.3 | async-start | bytes 294912 | tf_op jit(solution)/shard_map/all_to_all | solution.py:334

commit v5 on v4

--- a/solution.py
+++ b/solution.py
@@ -249,8 +249,8 @@
     quarter = own_gate.shape[1]
     parts = leave.shape[1]
     grad = kept[0].astype(F32) + crossed[0].astype(F32)
-    gate_grad = (grad * slope[...]).T.astype(BF16)
-    up_grad = (grad * active[...]).T.astype(BF16)
+    gate_grad = (grad * slope[...]).astype(BF16).T
+    up_grad = (grad * active[...]).astype(BF16).T
     stores = []
     for half, (gate, up) in enumerate(((own_gate, own_up), (far_gate, far_up))):
         for i, piece in enumerate(chunks(quarter, parts)):
@@ -291,6 +291,7 @@
     places = experts * CAP
     half = gate_weight.shape[1] * 2
     chunk = half // tensor
+    hidden_units = gate_weight.shape[2]
     own_gate, own_up, own_down = gate_weight[0].T, up_weight[0].T, down_weight[0]
 
     both = spread(x_rows, cotangent, tensor)
@@ -312,14 +313,16 @@
     got_dy = lax.all_gather(got[:, half : half + chunk].T, "tensor", axis=0, tiled=True)
     hidden_grad = project((own_down,), (far_down,), got_dy, 0, rows, True)
     crossed_grad = lax.ppermute(hidden_grad, "z_hi", SWAP)
-    swapped_dy = lax.ppermute(got_dy[half // 2 :], "core", SWAP)
 
     gate_up = gate_up.astype(F32) + crossed.astype(F32)
     gate, up = gate_up[0], gate_up[1]
     sigma = jax.nn.sigmoid(gate)
     active = gate * sigma
     hidden = (active * up).astype(BF16)
-    swapped_hidden = lax.ppermute(hidden, "core", SWAP)
+    swapped = lax.ppermute(
+        jnp.concatenate([hidden, got_dy[half // 2 :]], axis=0), "core", SWAP
+    )
+    swapped_hidden, swapped_dy = swapped[:hidden_units], swapped[hidden_units:]
     slope = up * sigma * (1.0 + gate * (1.0 - sigma))
 
     far_gate, far_up, _ = lax.optimization_barrier((far_gate, far_up, crossed))

time: 156 us -> 156 us (level)
  starting transfers between devices: 55.6 us -> 53.2 us
    ppermute x2 -> x1, starting transfers between devices: 4.33 us -> 1.92 us  [per_device(): lax.ppermute(jnp.concatenate([hidden, got_dy[half // 2:]], axis=0), 'core...]
    all_to_all x1, waiting for transfers between devices: 11 us -> 13.3 us  [per_device(): lax.all_to_all(term.reshape(2 * experts, CAP, half), SIDES, 0, 0, tiled=T...]
  transfers between devices with their start and end apart: 11 -> 10, of which waited for: 5 -> 5; matrix products, arithmetic and copies ran while one was open for 5% -> 5% of each run, Pallas kernels for 6% -> 6%
where the time goes in v5:
time: 156 us; the launch traced here: 155 us
  starting transfers between devices  53.2 us (34%)
  waiting for transfers between devices  50 us (32%)
  blocking collectives  26.1 us (17%)
  Pallas kernels  15.4 us (10%)
  other arithmetic  5.33 us (3%)
  matrix products  2.99 us (2%)
    all_gather x1, blocking collectives, per_device(): lax.all_gather(got[:, half:half + chunk].T, 'tensor', axis=0, tiled=True)  26.1 us
    all_to_all x1, waiting for transfers between devices, per_device(): lax.all_to_all(sent, SIDES, 0, 0, tiled=True)  16.2 us
    all_to_all x1, starting transfers between devices, per_device(): lax.all_to_all(sent, SIDES, 0, 0, tiled=True)  13.5 us
    all_to_all x1, waiting for transfers between devices, per_device(): lax.all_to_all(term.reshape(2 * experts, CAP, half), SIDES, 0, 0, tiled=T...  13.3 us
    all_to_all x1, starting transfers between devices, per_device(): lax.all_to_all(term.reshape(2 * experts, CAP, half), SIDES, 0, 0, tiled=T...  10.6 us
    all_to_all x1, waiting for transfers between devices, per_device(): both = lax.all_to_all(both, 'tensor', 0, 0, tiled=True)  8.13 us
    all_to_all x1, starting transfers between devices, per_device(): both = lax.all_to_all(both, 'tensor', 0, 0, tiled=True)  7.1 us
    pallas_call x2, Pallas kernels, project(): pl.pallas_call(functools.partial(project_body, pairs, side), in_specs=[hb...  6.81 us
  transfers between devices with their start and end apart: 10, of which 5 were waited for; matrix products, arithmetic and copies ran while one was open for 5% of the time, Pallas kernels for 6%

profile of v5, /device:TPU:2, one launch (start us, length us, event | category | flops | bytes accessed | tf_op | source)
XLA Modules:
  0.0 155.3 jit_solution(12156087379612420087)
XLA Ops:
  0.6 1.5 shard_map.86
  2.1 7.1 %all-to-all-start = ((bf16[8,24,640]{2,1,0:T(8,128)(2,1)}), bf16[8,24,640]{2,1,0:T(8,128)(2,1)S(1)}, u32[]{:S(2)}, u32[]{:S(2)}) async-start(bf16[8,24,640]{2,1,0:T(8,128)(2,1)} %shard_map.86), calls=%async_computation | async-start | bytes 491520 | tf_op jit(solution)/shard_map/all_to_all | solution.py:298
  9.2 0.7 convert_reduce_fusion.2
  10.1 0.7 select_reduce_fusion.1
  10.8 0.7 multiply_add_fusion
  11.5 0.8 select_reduce_fusion
  12.6 8.1 %all-to-all-done.tokens = bf16[8,24,640]{2,1,0:T(8,128)(2,1)S(1)} async-done(((bf16[8,24,640]{2,1,0:T(8,128)(2,1)}), bf16[8,24,640]{2,1,0:T(8,128)(2,1)S(1)}, u32[]{:S(2)}, u32[]{:S(2)}) %all-to-all-start) | async-done | bytes 245792 | tf_op jit(solution)/shard_map/all_to_all | solution.py:298
  20.8 1.7 %shard_map.87 = bf16[2,128,1792]{2,1,0:T(8,128)(2,1)} custom-call(s32[2]{0:T(128)S(1)} %pad_add_fusion.place, bf16[8,24,640]{2,1,0:T(8,128)(2,1)S(1)} %all-to-all-done.tokens, bf16[128,24]{1,0:T(8,128)(2,1)S(1)} %copy.27.gather, f32[128,1]{1,0:T(8,128)S(1)} %copy.28.slot_weight), custom_call_target="tpu_custom_call" | custom-call | flops 18874368 | bytes 1600000 | tf_op jit(solution)/shard_map/pallas_call | solution.py:111
  22.5 13.5 %all-to-all-start.1 = ((bf16[32,8,1792]{2,1,0:T(8,128)(2,1)}), bf16[32,8,1792]{2,1,0:T(8,128)(2,1)S(1)}, u32[]{:S(2)}, u32[]{:S(2)}) async-start(bf16[32,8,1792]{2,1,0:T(8,128)(2,1)} %bitcast.44), calls=%async_computation.1 | async-start | bytes 1835008 | tf_op jit(solution)/shard_map/all_to_all | solution.py:308
  36.0 1.9 %collective-permute-start.2 = (bf16[672,768]{1,0:T(8,128)(2,1)S(1)}, bf16[672,768]{1,0:T(8,128)(2,1)S(1)}, u32[]{:S(2)}, u32[]{:S(2)}) collective-permute-start(bf16[672,768]{1,0:T(8,128)(2,1)S(1)} %bitcast.37), channel_id=1, source_target_pairs={{0,128},{128,0},{1,129},{129,1},{2,130},{130,2},{3,131},{131,3},{4... | collective-permute-start | bytes 3096584 | tf_op jit(solution)/shard_map/ppermute | solution.py:302
  37.9 2.4 %collective-permute-start.3 = (bf16[672,768]{1,0:T(8,128)(2,1)S(1)}, bf16[672,768]{1,0:T(8,128)(2,1)}, u32[]{:S(2)}, u32[]{:S(2)}) collective-permute-start(bf16[672,768]{1,0:T(8,128)(2,1)S(1)} %bitcast.40), channel_id=1, source_target_pairs={{0,128},{128,0},{1,129},{129,1},{2,130},{130,2},{3,131},{131,3},{4... | collective-permute-start | bytes 3096584 | tf_op jit(solution)/shard_map/ppermute | solution.py:303
  40.3 1.9 %collective-permute-start = (bf16[672,768]{1,0:T(8,128)(2,1)}, bf16[672,768]{1,0:T(8,128)(2,1)}, u32[]{:S(2)}, u32[]{:S(2)}) collective-permute-start(bf16[672,768]{1,0:T(8,128)(2,1)} %bitcast.46), channel_id=1, source_target_pairs={{0,128},{128,0},{1,129},{129,1},{2,130},{130,2},{3,131},{131,3},{4... | collective-permute-start | bytes 3096584 | tf_op jit(solution)/shard_map/ppermute | solution.py:304
  42.3 1.0 copy-done.3
  43.3 16.2 %all-to-all-done.1 = bf16[32,8,1792]{2,1,0:T(8,128)(2,1)S(1)} async-done(((bf16[32,8,1792]{2,1,0:T(8,128)(2,1)}), bf16[32,8,1792]{2,1,0:T(8,128)(2,1)S(1)}, u32[]{:S(2)}, u32[]{:S(2)}) %all-to-all-start.1) | async-done | bytes 917536 | tf_op jit(solution)/shard_map/all_to_all | solution.py:308
  59.4 3.6 %shard_map.89 = bf16[2,672,256]{2,1,0:T(8,128)(2,1)} custom-call(bf16[672,768]{1,0:T(8,128)(2,1)S(1)} %bitcast.38, bf16[672,768]{1,0:T(8,128)(2,1)S(1)} %bitcast.41, bf16[672,768]{1,0:T(8,128)(2,1)} %copy-done.3, bf16[672,768]{1,0:T(8,128)(2,1)} %collective-permute-done.3.refs_3_.refs_1_, bf16[256,1792]{1,0:T(8,128)(2,1)S(1)} %bitcast.35), custom_call_target="tpu_custom_call" | custom-call | flops 1056964608 | bytes 4128768 | tf_op jit(solution)/shard_map/pallas_call | solution.py:229
  63.0 3.4 %collective-permute-start.4 = (bf16[2,672,256]{2,1,0:T(8,128)(2,1)}, bf16[2,672,256]{2,1,0:T(8,128)(2,1)}, u32[]{:S(2)}, u32[]{:S(2)}) collective-permute-start(bf16[2,672,256]{2,1,0:T(8,128)(2,1)} %shard_map.89), channel_id=1, source_target_pairs={{0,256},{256,0},{1,257},{257,1},{2,258},{258,2},{3,259},{259,3},{4... | collective-permute-start | bytes 2064392 | tf_op jit(solution)/shard_map/ppermute | solution.py:312
  66.5 26.1 %all_gather.3.refs_2_ = bf16[1536,256]{1,0:T(8,128)(2,1)S(1)} all-gather(bf16[192,256]{1,0:T(8,128)(2,1)S(1)} %copy.29), channel_id=1, replica_groups=mesh['z_hi'=2,'core'=2,'z_lo'=4,'x'=4,'tensor'=8] {'tensor'}, dimensions={0}, use_global_device_ids=true | all-gather | bytes 884736 | tf_op jit(solution)/shard_map/all_gather | solution.py:313
  92.6 3.3 %shard_map.88.kept = bf16[1,672,256]{2,1,0:T(8,128)(2,1)} custom-call(bf16[672,768]{1,0:T(8,128)(2,1)} %bitcast.47, bf16[672,768]{1,0:T(8,128)(2,1)} %collective-permute-done.refs_1_, bf16[1536,256]{1,0:T(8,128)(2,1)S(1)} %all_gather.3.refs_2_), custom_call_target="tpu_custom_call" | custom-call | flops 528482304 | bytes 2064384 | tf_op jit(solution)/shard_map/pallas_call | solution.py:229
  95.8 6.5 %collective-permute-start.1 = (bf16[1,672,256]{2,1,0:T(8,128)(2,1)}, bf16[1,672,256]{2,1,0:T(8,128)(2,1)S(1)}, u32[]{:S(2)}, u32[]{:S(2)}) collective-permute-start(bf16[1,672,256]{2,1,0:T(8,128)(2,1)} %shard_map.88.kept), channel_id=1, source_target_pairs={{0,256},{256,0},{1,257},{257,1},{2,258},{258,2},{3,259},{259,3},{4... | collective-permute-start | bytes 1032200 | tf_op jit(solution)/shard_map/ppermute | solution.py:315
  102.4 1.2 convert_add_fusion
  103.6 1.7 %shard_map.90 = (bf16[672,768]{1,0:T(8,128)(2,1)S(1)}, bf16[672,768]{1,0:T(8,128)(2,1)S(1)}) custom-call(bf16[672,768]{1,0:T(8,128)(2,1)} %copy-done.3, bf16[672,768]{1,0:T(8,128)(2,1)} %collective-permute-done.3.refs_3_.refs_1_), custom_call_target="tpu_custom_call" | custom-call | bytes 4000000 | tf_op jit(solution)/shard_map/pallas_call | solution.py:169
  105.6 6.1 %collective-permute-done.1.crossed = bf16[1,672,256]{2,1,0:T(8,128)(2,1)S(1)} collective-permute-done((bf16[1,672,256]{2,1,0:T(8,128)(2,1)}, bf16[1,672,256]{2,1,0:T(8,128)(2,1)S(1)}, u32[]{:S(2)}, u32[]{:S(2)}) %collective-permute-start.1) | collective-permute-done | bytes 344096 | tf_op jit(solution)/shard_map/ppermute | solution.py:315
  111.8 2.2 %shard_map.91 = bf16[256,1536]{1,0:T(8,128)(2,1)} custom-call(bf16[1,672,256]{2,1,0:T(8,128)(2,1)S(1)} %copy-done.2, bf16[1,672,256]{2,1,0:T(8,128)(2,1)S(1)} %collective-permute-done.1.crossed, f32[672,256]{1,0:T(8,128)S(1)} %get-tuple-element.14.slope, f32[672,256]{1,0:T(8,128)S(1)} %get-tuple-element.13.active, bf16[672,768]{1,0:T(8,128)(2,1)S(1)} %bitcast.39, ...), custom_call_target="tpu_custom_call" | custom-call | flops 1056964608 | bytes 4128768 | tf_op jit(solution)/shard_map/pallas_call | solution.py:273
  114.0 10.6 %all-to-all-start.2 = ((bf16[32,8,1536]{2,1,0:T(8,128)(2,1)}), bf16[32,8,1536]{2,1,0:T(8,128)(2,1)S(1)}, u32[]{:S(2)}, u32[]{:S(2)}) async-start(bf16[32,8,1536]{2,1,0:T(8,128)(2,1)} %bitcast.45), calls=%async_computation.2 | async-start | bytes 1572864 | tf_op jit(solution)/shard_map/all_to_all | solution.py:333
  124.7 1.9 %collective-permute-start.5 = (bf16[1440,256]{1,0:T(8,128)(2,1)S(1)}, bf16[1440,256]{1,0:T(8,128)(2,1)}, u32[]{:S(2)}, u32[]{:S(2)}) collective-permute-start(bf16[1440,256]{1,0:T(8,128)(2,1)S(1)} %pad_maximum_fusion), channel_id=1, source_target_pairs={{0,128},{128,0},{1,129},{129,1},{2,130},{130,2},{3,131},{131,3},{4... | collective-permute-start | bytes 2211848 | tf_op jit(solution)/shard_map/ppermute | solution.py:322
  126.7 13.3 %all-to-all-done.2 = bf16[32,8,1536]{2,1,0:T(8,128)(2,1)S(1)} async-done(((bf16[32,8,1536]{2,1,0:T(8,128)(2,1)}), bf16[32,8,1536]{2,1,0:T(8,128)(2,1)S(1)}, u32[]{:S(2)}, u32[]{:S(2)}) %all-to-all-start.2) | async-done | bytes 786464 | tf_op jit(solution)/shard_map/all_to_all | solution.py:333
  140.0 1.5 shard_map.92
  141.5 4.0 %all-to-all-start.3 = ((bf16[8,24,384]{2,1,0:T(8,128)(2,1)}), bf16[8,24,384]{2,1,0:T(8,128)(2,1)S(1)}, u32[]{:S(2)}, u32[]{:S(2)}) async-start(bf16[8,24,384]{2,1,0:T(8,128)(2,1)} %shard_map.92), calls=%async_computation.3 | async-start | bytes 294912 | tf_op jit(solution)/shard_map/all_to_all | solution.py:337
  145.4 0.5 fusion.3
  145.9 2.5 %fusion = bf16[1,672,768]{2,1,0:T(8,128)(2,1)} fusion(f32[672,768]{1,0:T(8,128)S(1)} %fusion.3, bf16[1440,256]{1,0:T(8,128)(2,1)} %collective-permute-done.5), kind=kOutput, calls=%fused_computation.2 | convolution fusion | flops 265273344 | bytes 3833856 | tf_op jit(solution)/shard_map/dot_general | solution.py:37
  148.4 6.2 %all-to-all-done.3 = bf16[8,24,384]{2,1,0:T(8,128)(2,1)S(1)} async-done(((bf16[8,24,384]{2,1,0:T(8,128)(2,1)}), bf16[8,24,384]{2,1,0:T(8,128)(2,1)S(1)}, u32[]{:S(2)}, u32[]{:S(2)}) %all-to-all-start.3) | async-done | bytes 147488 | tf_op jit(solution)/shard_map/all_to_all | solution.py:337
  154.7 0.6 reduce_sum.62
  (27 shorter events, 1.1 us)
Async XLA Ops:
  2.1 18.6 %all-to-all-start = ((bf16[8,24,640]{2,1,0:T(8,128)(2,1)}), bf16[8,24,640]{2,1,0:T(8,128)(2,1)S(1)}, u32[]{:S(2)}, u32[]{:S(2)}) async-start(bf16[8,24,640]{2,1,0:T(8,128)(2,1)} %shard_map.86), calls=%async_computation | async-start | bytes 491520 | tf_op jit(solution)/shard_map/all_to_all | solution.py:298
  12.6 23.4 %copy-start = (bf16[1,768,672]{1,2,0:T(8,128)(2,1)S(1)}, bf16[1,768,672]{1,2,0:T(8,128)(2,1)}, u32[]{:S(2)}) copy-start(bf16[1,768,672]{1,2,0:T(8,128)(2,1)} %param.11) | copy-start | bytes 3096580
  12.6 25.3 %copy-start.1 = (bf16[1,768,672]{1,2,0:T(8,128)(2,1)S(1)}, bf16[1,768,672]{1,2,0:T(8,128)(2,1)}, u32[]{:S(2)}) copy-start(bf16[1,768,672]{1,2,0:T(8,128)(2,1)} %param.12) | copy-start | bytes 3096580
  22.5 36.9 %all-to-all-start.1 = ((bf16[32,8,1792]{2,1,0:T(8,128)(2,1)}), bf16[32,8,1792]{2,1,0:T(8,128)(2,1)S(1)}, u32[]{:S(2)}, u32[]{:S(2)}) async-start(bf16[32,8,1792]{2,1,0:T(8,128)(2,1)} %bitcast.44), calls=%async_computation.1 | async-start | bytes 1835008 | tf_op jit(solution)/shard_map/all_to_all | solution.py:308
  36.0 6.3 %collective-permute-start.2 = (bf16[672,768]{1,0:T(8,128)(2,1)S(1)}, bf16[672,768]{1,0:T(8,128)(2,1)S(1)}, u32[]{:S(2)}, u32[]{:S(2)}) collective-permute-start(bf16[672,768]{1,0:T(8,128)(2,1)S(1)} %bitcast.37), channel_id=1, source_target_pairs={{0,128},{128,0},{1,129},{129,1},{2,130},{130,2},{3,131},{131,3},{4... | collective-permute-start | bytes 3096584 | tf_op jit(solution)/shard_map/ppermute | solution.py:302
  37.9 5.3 %collective-permute-start.3 = (bf16[672,768]{1,0:T(8,128)(2,1)S(1)}, bf16[672,768]{1,0:T(8,128)(2,1)}, u32[]{:S(2)}, u32[]{:S(2)}) collective-permute-start(bf16[672,768]{1,0:T(8,128)(2,1)S(1)} %bitcast.40), channel_id=1, source_target_pairs={{0,128},{128,0},{1,129},{129,1},{2,130},{130,2},{3,131},{131,3},{4... | collective-permute-start | bytes 3096584 | tf_op jit(solution)/shard_map/ppermute | solution.py:303
  40.3 52.2 %collective-permute-start = (bf16[672,768]{1,0:T(8,128)(2,1)}, bf16[672,768]{1,0:T(8,128)(2,1)}, u32[]{:S(2)}, u32[]{:S(2)}) collective-permute-start(bf16[672,768]{1,0:T(8,128)(2,1)} %bitcast.46), channel_id=1, source_target_pairs={{0,128},{128,0},{1,129},{129,1},{2,130},{130,2},{3,131},{131,3},{4... | collective-permute-start | bytes 3096584 | tf_op jit(solution)/shard_map/ppermute | solution.py:304
  42.3 1.0 copy-start.3
  63.0 39.4 %collective-permute-start.4 = (bf16[2,672,256]{2,1,0:T(8,128)(2,1)}, bf16[2,672,256]{2,1,0:T(8,128)(2,1)}, u32[]{:S(2)}, u32[]{:S(2)}) collective-permute-start(bf16[2,672,256]{2,1,0:T(8,128)(2,1)} %shard_map.89), channel_id=1, source_target_pairs={{0,256},{256,0},{1,257},{257,1},{2,258},{258,2},{3,259},{259,3},{4... | collective-permute-start | bytes 2064392 | tf_op jit(solution)/shard_map/ppermute | solution.py:312
  92.5 9.8 %copy-start.4 = (bf16[2,672,256]{2,1,0:T(8,128)(2,1)S(1)}, bf16[2,672,256]{2,1,0:T(8,128)(2,1)}, u32[]{:S(2)}) copy-start(bf16[2,672,256]{2,1,0:T(8,128)(2,1)} %shard_map.89) | copy-start | bytes 2064388
  95.8 15.9 %collective-permute-start.1 = (bf16[1,672,256]{2,1,0:T(8,128)(2,1)}, bf16[1,672,256]{2,1,0:T(8,128)(2,1)S(1)}, u32[]{:S(2)}, u32[]{:S(2)}) collective-permute-start(bf16[1,672,256]{2,1,0:T(8,128)(2,1)} %shard_map.88.kept), channel_id=1, source_target_pairs={{0,256},{256,0},{1,257},{257,1},{2,258},{258,2},{3,259},{259,3},{4... | collective-permute-start | bytes 1032200 | tf_op jit(solution)/shard_map/ppermute | solution.py:315
  105.3 6.5 %copy-start.2 = (bf16[1,672,256]{2,1,0:T(8,128)(2,1)S(1)}, bf16[1,672,256]{2,1,0:T(8,128)(2,1)}, u32[]{:S(2)}) copy-start(bf16[1,672,256]{2,1,0:T(8,128)(2,1)} %shard_map.88.kept) | copy-start | bytes 1032196
  114.0 26.0 %all-to-all-start.2 = ((bf16[32,8,1536]{2,1,0:T(8,128)(2,1)}), bf16[32,8,1536]{2,1,0:T(8,128)(2,1)S(1)}, u32[]{:S(2)}, u32[]{:S(2)}) async-start(bf16[32,8,1536]{2,1,0:T(8,128)(2,1)} %bitcast.45), calls=%async_computation.2 | async-start | bytes 1572864 | tf_op jit(solution)/shard_map/all_to_all | solution.py:333
  124.7 21.2 %collective-permute-start.5 = (bf16[1440,256]{1,0:T(8,128)(2,1)S(1)}, bf16[1440,256]{1,0:T(8,128)(2,1)}, u32[]{:S(2)}, u32[]{:S(2)}) collective-permute-start(bf16[1440,256]{1,0:T(8,128)(2,1)S(1)} %pad_maximum_fusion), channel_id=1, source_target_pairs={{0,128},{128,0},{1,129},{129,1},{2,130},{130,2},{3,131},{131,3},{4... | collective-permute-start | bytes 2211848 | tf_op jit(solution)/shard_map/ppermute | solution.py:322
  141.5 13.2 %all-to-all-start.3 = ((bf16[8,24,384]{2,1,0:T(8,128)(2,1)}), bf16[8,24,384]{2,1,0:T(8,128)(2,1)S(1)}, u32[]{:S(2)}, u32[]{:S(2)}) async-start(bf16[8,24,384]{2,1,0:T(8,128)(2,1)} %shard_map.92), calls=%async_computation.3 | async-start | bytes 294912 | tf_op jit(solution)/shard_map/all_to_all | solution.py:337

commit v6 on v5

--- a/solution.py
+++ b/solution.py
@@ -177,7 +177,7 @@
 
 
 def project_body(pairs, side, *refs):
-    own, far, (act, out, fetched, partial, held, arrive, leave) = (
+    own, far, (act, out, turned, fetched, partial, held, arrive, leave) = (
         refs[:pairs],
         refs[pairs : 2 * pairs],
         refs[2 * pairs :],
@@ -205,6 +205,10 @@
                 loads[p][i].wait()
             rows = fetched[p, piece] if fetch_own else own[p][piece]
             partial[p, piece] = dot(rows, near, 1, side)
+    if side == 1:
+        turned[...] = act[:, 2 * quarter :].T[: turned.shape[0]]
+    else:
+        turned[...] = jnp.zeros_like(turned)
     stores = []
     shift = pairs if fetch_own else 0
     for p in range(pairs):
@@ -220,7 +224,7 @@
         store.wait()
 
 
-def project(own, far, act, side, count, fetch_own):
+def project(own, far, act, side, count, fetch_own, tail=16):
     pairs = len(own)
     hidden, quarter = own[0].shape
     parts = 2
@@ -229,8 +233,11 @@
     return pl.pallas_call(
         functools.partial(project_body, pairs, side),
         in_specs=[hbm if fetch_own else vmem] * pairs + [hbm] * pairs + [vmem],
-        out_specs=hbm,
-        out_shape=pltpu.HBM((pairs, hidden, count), BF16),
+        out_specs=[hbm, vmem],
+        out_shape=[
+            pltpu.HBM((pairs, hidden, count), BF16),
+            jax.ShapeDtypeStruct((tail, count), BF16),
+        ],
         scratch_shapes=[
             pltpu.VMEM((fetched, hidden, quarter), BF16),
             pltpu.VMEM((pairs, hidden, count), F32),
@@ -308,10 +315,10 @@
     got = lax.all_to_all(sent, SIDES, 0, 0, tiled=True).reshape(2 * places, half + 256)
 
     rows = 2 * places
-    gate_up = project((own_gate, own_up), (far_gate, far_up), got, 1, rows, False)
+    gate_up, dy_chunk = project((own_gate, own_up), (far_gate, far_up), got, 1, rows, False, chunk)
     crossed = lax.ppermute(gate_up, "z_hi", SWAP)
-    got_dy = lax.all_gather(got[:, half : half + chunk].T, "tensor", axis=0, tiled=True)
-    hidden_grad = project((own_down,), (far_down,), got_dy, 0, rows, True)
+    got_dy = lax.all_gather(dy_chunk, "tensor", axis=0, tiled=True)
+    hidden_grad, _ = project((own_down,), (far_down,), got_dy, 0, rows, True)
     crossed_grad = lax.ppermute(hidden_grad, "z_hi", SWAP)
 
     gate_up = gate_up.astype(F32) + crossed.astype(F32)

time: 156 us -> 157 us (level)
  Pallas kernels: 15.4 us -> 17.2 us
    pallas_call x2, Pallas kernels: 6.81 us -> 8.58 us  [project(): pl.pallas_call(functools.partial(project_body, pairs, side), in_specs=[hb...]
  transfers between devices with their start and end apart: 10 -> 10, of which waited for: 5 -> 5; matrix products, arithmetic and copies ran while one was open for 5% -> 4% of each run, Pallas kernels for 6% -> 7%
where the time goes in v6:
time: 157 us
  starting transfers between devices  52.8 us (34%)
  waiting for transfers between devices  51 us (32%)
  blocking collectives  26.1 us (17%)
  Pallas kernels  17.2 us (11%)
  other arithmetic  4.23 us (3%)
  matrix products  3 us (2%)
    all_gather x1, blocking collectives, per_device(): got_dy = lax.all_gather(dy_chunk, 'tensor', axis=0, tiled=True)  26.1 us
    all_to_all x1, waiting for transfers between devices, per_device(): lax.all_to_all(sent, SIDES, 0, 0, tiled=True)  16.2 us
    all_to_all x1, starting transfers between devices, per_device(): lax.all_to_all(sent, SIDES, 0, 0, tiled=True)  13.5 us
    all_to_all x1, waiting for transfers between devices, per_device(): lax.all_to_all(term.reshape(2 * experts, CAP, half), SIDES, 0, 0, tiled=T...  13.3 us
    all_to_all x1, starting transfers between devices, per_device(): lax.all_to_all(term.reshape(2 * experts, CAP, half), SIDES, 0, 0, tiled=T...  10.2 us
    pallas_call x2, Pallas kernels, project(): pl.pallas_call(functools.partial(project_body, pairs, side), in_specs=[hb...  8.58 us
    all_to_all x1, waiting for transfers between devices, per_device(): both = lax.all_to_all(both, 'tensor', 0, 0, tiled=True)  8.13 us
    all_to_all x1, starting transfers between devices, per_device(): both = lax.all_to_all(both, 'tensor', 0, 0, tiled=True)  7.1 us
  transfers between devices with their start and end apart: 10, of which 5 were waited for; matrix products, arithmetic and copies ran while one was open for 4% of the time, Pallas kernels for 7%

profile of v6, /device:TPU:2, one launch (start us, length us, event | category | flops | bytes accessed | tf_op | source)
XLA Modules:
  0.0 156.5 jit_solution(15271480763176316614)
XLA Ops:
  0.6 1.5 shard_map.86
  2.1 7.1 %all-to-all-start = ((bf16[8,24,640]{2,1,0:T(8,128)(2,1)}), bf16[8,24,640]{2,1,0:T(8,128)(2,1)S(1)}, u32[]{:S(2)}, u32[]{:S(2)}) async-start(bf16[8,24,640]{2,1,0:T(8,128)(2,1)} %shard_map.86), calls=%async_computation | async-start | bytes 491520 | tf_op jit(solution)/shard_map/all_to_all | solution.py:305
  9.2 0.7 convert_reduce_fusion.2
  10.1 0.7 select_reduce_fusion.1
  10.8 0.7 multiply_add_fusion
  11.5 0.8 select_reduce_fusion
  12.6 8.1 %all-to-all-done.tokens = bf16[8,24,640]{2,1,0:T(8,128)(2,1)S(1)} async-done(((bf16[8,24,640]{2,1,0:T(8,128)(2,1)}), bf16[8,24,640]{2,1,0:T(8,128)(2,1)S(1)}, u32[]{:S(2)}, u32[]{:S(2)}) %all-to-all-start) | async-done | bytes 245792 | tf_op jit(solution)/shard_map/all_to_all | solution.py:305
  20.8 1.7 %shard_map.87 = bf16[2,128,1792]{2,1,0:T(8,128)(2,1)} custom-call(s32[2]{0:T(128)S(1)} %pad_add_fusion.place, bf16[8,24,640]{2,1,0:T(8,128)(2,1)S(1)} %all-to-all-done.tokens, bf16[128,24]{1,0:T(8,128)(2,1)S(1)} %copy.20.gather, f32[128,1]{1,0:T(8,128)S(1)} %copy.21.slot_weight), custom_call_target="tpu_custom_call" | custom-call | flops 18874368 | bytes 1600000 | tf_op jit(solution)/shard_map/pallas_call | solution.py:111
  22.5 13.5 %all-to-all-start.1 = ((bf16[32,8,1792]{2,1,0:T(8,128)(2,1)}), bf16[32,8,1792]{2,1,0:T(8,128)(2,1)}, u32[]{:S(2)}, u32[]{:S(2)}) async-start(bf16[32,8,1792]{2,1,0:T(8,128)(2,1)} %bitcast.40), calls=%async_computation.1 | async-start | bytes 1835008 | tf_op jit(solution)/shard_map/all_to_all | solution.py:315
  36.0 1.9 %collective-permute-start.1 = (bf16[672,768]{1,0:T(8,128)(2,1)S(1)}, bf16[672,768]{1,0:T(8,128)(2,1)S(1)}, u32[]{:S(2)}, u32[]{:S(2)}) collective-permute-start(bf16[672,768]{1,0:T(8,128)(2,1)S(1)} %bitcast.33), channel_id=1, source_target_pairs={{0,128},{128,0},{1,129},{129,1},{2,130},{130,2},{3,131},{131,3},{4... | collective-permute-start | bytes 3096584 | tf_op jit(solution)/shard_map/ppermute | solution.py:309
  38.0 2.4 %collective-permute-start.2 = (bf16[672,768]{1,0:T(8,128)(2,1)S(1)}, bf16[672,768]{1,0:T(8,128)(2,1)}, u32[]{:S(2)}, u32[]{:S(2)}) collective-permute-start(bf16[672,768]{1,0:T(8,128)(2,1)S(1)} %bitcast.36), channel_id=1, source_target_pairs={{0,128},{128,0},{1,129},{129,1},{2,130},{130,2},{3,131},{131,3},{4... | collective-permute-start | bytes 3096584 | tf_op jit(solution)/shard_map/ppermute | solution.py:310
  40.4 1.9 %collective-permute-start = (bf16[672,768]{1,0:T(8,128)(2,1)}, bf16[672,768]{1,0:T(8,128)(2,1)}, u32[]{:S(2)}, u32[]{:S(2)}) collective-permute-start(bf16[672,768]{1,0:T(8,128)(2,1)} %bitcast.2.refs_0_), channel_id=1, source_target_pairs={{0,128},{128,0},{1,129},{129,1},{2,130},{130,2},{3,131},{131,3},{4... | collective-permute-start | bytes 3096584 | tf_op jit(solution)/shard_map/ppermute | solution.py:311
  42.4 1.0 copy-done.3
  43.3 16.2 %all-to-all-done.1 = bf16[32,8,1792]{2,1,0:T(8,128)(2,1)} async-done(((bf16[32,8,1792]{2,1,0:T(8,128)(2,1)}), bf16[32,8,1792]{2,1,0:T(8,128)(2,1)}, u32[]{:S(2)}, u32[]{:S(2)}) %all-to-all-start.1) | async-done | bytes 917536 | tf_op jit(solution)/shard_map/all_to_all | solution.py:315
  59.5 4.7 %shard_map.88 = (bf16[2,672,256]{2,1,0:T(8,128)(2,1)}, bf16[192,256]{1,0:T(8,128)(2,1)S(1)}) custom-call(bf16[672,768]{1,0:T(8,128)(2,1)S(1)} %bitcast.34, bf16[672,768]{1,0:T(8,128)(2,1)S(1)} %bitcast.37, bf16[672,768]{1,0:T(8,128)(2,1)} %copy-done.3, bf16[672,768]{1,0:T(8,128)(2,1)} %collective-permute-done.2.refs_3_.refs_1_, ...), custom_call_target="tpu_custom_call" | custom-call | flops 1056964608 | bytes 4128768 | tf_op jit(solution)/shard_map/pallas_call | solution.py:233
  64.3 3.4 %collective-permute-start.4 = (bf16[2,672,256]{2,1,0:T(8,128)(2,1)}, bf16[2,672,256]{2,1,0:T(8,128)(2,1)S(1)}, u32[]{:S(2)}, u32[]{:S(2)}) collective-permute-start(bf16[2,672,256]{2,1,0:T(8,128)(2,1)} %get-tuple-element.11), channel_id=1, source_target_pairs={{0,256},{256,0},{1,257},{257,1},{2,258},{258,2},{3,259},{259,3},{4... | collective-permute-start | bytes 2064392 | tf_op jit(solution)/shard_map/ppermute | solution.py:319
  67.7 26.1 %all_gather.3.refs_2_ = bf16[1536,256]{1,0:T(8,128)(2,1)S(1)} all-gather(bf16[192,256]{1,0:T(8,128)(2,1)S(1)} %get-tuple-element.9), channel_id=1, replica_groups=mesh['z_hi'=2,'core'=2,'z_lo'=4,'x'=4,'tensor'=8] {'tensor'}, dimensions={0}, use_global_device_ids=true | all-gather | bytes 884736 | tf_op jit(solution)/shard_map/all_gather | solution.py:320
  93.8 3.8 %shard_map.89 = (bf16[1,672,256]{2,1,0:T(8,128)(2,1)}, bf16[16,256]{1,0:T(8,128)(2,1)}) custom-call(bf16[672,768]{1,0:T(8,128)(2,1)} %bitcast.2.refs_0_, bf16[672,768]{1,0:T(8,128)(2,1)} %collective-permute-done.refs_1_, bf16[1536,256]{1,0:T(8,128)(2,1)S(1)} %all_gather.3.refs_2_), custom_call_target="tpu_custom_call" | custom-call | flops 528482304 | bytes 2064384 | tf_op jit(solution)/shard_map/pallas_call | solution.py:233
  97.6 6.5 %collective-permute-start.3 = (bf16[1,672,256]{2,1,0:T(8,128)(2,1)}, bf16[1,672,256]{2,1,0:T(8,128)(2,1)S(1)}, u32[]{:S(2)}, u32[]{:S(2)}) collective-permute-start(bf16[1,672,256]{2,1,0:T(8,128)(2,1)} %get-tuple-element.10.kept), channel_id=1, source_target_pairs={{0,256},{256,0},{1,257},{257,1},{2,258},{258,2},{3,259},{259,3},{4... | collective-permute-start | bytes 1032200 | tf_op jit(solution)/shard_map/ppermute | solution.py:322
  104.4 1.7 %shard_map.90 = (bf16[672,768]{1,0:T(8,128)(2,1)S(1)}, bf16[672,768]{1,0:T(8,128)(2,1)S(1)}) custom-call(bf16[672,768]{1,0:T(8,128)(2,1)} %copy-done.3, bf16[672,768]{1,0:T(8,128)(2,1)} %collective-permute-done.2.refs_3_.refs_1_), custom_call_target="tpu_custom_call" | custom-call | bytes 4000000 | tf_op jit(solution)/shard_map/pallas_call | solution.py:169
  106.0 0.3 multiply_convert_fusion
  106.4 7.0 %collective-permute-done.3.crossed = bf16[1,672,256]{2,1,0:T(8,128)(2,1)S(1)} collective-permute-done((bf16[1,672,256]{2,1,0:T(8,128)(2,1)}, bf16[1,672,256]{2,1,0:T(8,128)(2,1)S(1)}, u32[]{:S(2)}, u32[]{:S(2)}) %collective-permute-start.3) | collective-permute-done | bytes 344096 | tf_op jit(solution)/shard_map/ppermute | solution.py:322
  113.4 2.2 %shard_map.91 = bf16[256,1536]{1,0:T(8,128)(2,1)} custom-call(bf16[1,672,256]{2,1,0:T(8,128)(2,1)S(1)} %copy-done.2, bf16[1,672,256]{2,1,0:T(8,128)(2,1)S(1)} %collective-permute-done.3.crossed, f32[672,256]{1,0:T(8,128)S(1)} %get-tuple-element.20.slope, f32[672,256]{1,0:T(8,128)S(1)} %get-tuple-element.19.active, bf16[672,768]{1,0:T(8,128)(2,1)S(1)} %bitcast.35, ...), custom_call_target="tpu_custom_call" | custom-call | flops 1056964608 | bytes 4128768 | tf_op jit(solution)/shard_map/pallas_call | solution.py:280
  115.7 10.2 %all-to-all-start.2 = ((bf16[32,8,1536]{2,1,0:T(8,128)(2,1)}), bf16[32,8,1536]{2,1,0:T(8,128)(2,1)S(1)}, u32[]{:S(2)}, u32[]{:S(2)}) async-start(bf16[32,8,1536]{2,1,0:T(8,128)(2,1)} %bitcast.41), calls=%async_computation.2 | async-start | bytes 1572864 | tf_op jit(solution)/shard_map/all_to_all | solution.py:340
  126.0 1.9 %collective-permute-start.5 = (bf16[1440,256]{1,0:T(8,128)(2,1)S(1)}, bf16[1440,256]{1,0:T(8,128)(2,1)}, u32[]{:S(2)}, u32[]{:S(2)}) collective-permute-start(bf16[1440,256]{1,0:T(8,128)(2,1)S(1)} %pad_maximum_fusion), channel_id=1, source_target_pairs={{0,128},{128,0},{1,129},{129,1},{2,130},{130,2},{3,131},{131,3},{4... | collective-permute-start | bytes 2211848 | tf_op jit(solution)/shard_map/ppermute | solution.py:329
  128.0 13.3 %all-to-all-done.2 = bf16[32,8,1536]{2,1,0:T(8,128)(2,1)S(1)} async-done(((bf16[32,8,1536]{2,1,0:T(8,128)(2,1)}), bf16[32,8,1536]{2,1,0:T(8,128)(2,1)S(1)}, u32[]{:S(2)}, u32[]{:S(2)}) %all-to-all-start.2) | async-done | bytes 786464 | tf_op jit(solution)/shard_map/all_to_all | solution.py:340
  141.3 1.5 shard_map.92
  142.8 3.9 %all-to-all-start.3 = ((bf16[8,24,384]{2,1,0:T(8,128)(2,1)}), bf16[8,24,384]{2,1,0:T(8,128)(2,1)S(1)}, u32[]{:S(2)}, u32[]{:S(2)}) async-start(bf16[8,24,384]{2,1,0:T(8,128)(2,1)} %shard_map.92), calls=%async_computation.3 | async-start | bytes 294912 | tf_op jit(solution)/shard_map/all_to_all | solution.py:344
  146.6 1.6 %fusion.2 = f32[672,768]{1,0:T(8,128)S(1)} fusion(bf16[1440,256]{1,0:T(8,128)(2,1)} %collective-permute-done.5), kind=kOutput, calls=%fused_computation.10 | convolution fusion | flops 264241152 | bytes 2801664 | tf_op jit(solution)/shard_map/dot_general | solution.py:37
  148.2 1.4 fusion
  149.6 6.2 %all-to-all-done.3 = bf16[8,24,384]{2,1,0:T(8,128)(2,1)S(1)} async-done(((bf16[8,24,384]{2,1,0:T(8,128)(2,1)}), bf16[8,24,384]{2,1,0:T(8,128)(2,1)S(1)}, u32[]{:S(2)}, u32[]{:S(2)}) %all-to-all-start.3) | async-done | bytes 147488 | tf_op jit(solution)/shard_map/all_to_all | solution.py:344
  155.9 0.6 reduce_sum.62
  (25 shorter events, 0.8 us)
Async XLA Ops:
  2.1 18.6 %all-to-all-start = ((bf16[8,24,640]{2,1,0:T(8,128)(2,1)}), bf16[8,24,640]{2,1,0:T(8,128)(2,1)S(1)}, u32[]{:S(2)}, u32[]{:S(2)}) async-start(bf16[8,24,640]{2,1,0:T(8,128)(2,1)} %shard_map.86), calls=%async_computation | async-start | bytes 491520 | tf_op jit(solution)/shard_map/all_to_all | solution.py:305
  12.6 23.4 %copy-start = (bf16[1,768,672]{1,2,0:T(8,128)(2,1)S(1)}, bf16[1,768,672]{1,2,0:T(8,128)(2,1)}, u32[]{:S(2)}) copy-start(bf16[1,768,672]{1,2,0:T(8,128)(2,1)} %param.11) | copy-start | bytes 3096580
  12.6 25.3 %copy-start.1 = (bf16[1,768,672]{1,2,0:T(8,128)(2,1)S(1)}, bf16[1,768,672]{1,2,0:T(8,128)(2,1)}, u32[]{:S(2)}) copy-start(bf16[1,768,672]{1,2,0:T(8,128)(2,1)} %param.12) | copy-start | bytes 3096580
  22.5 37.0 %all-to-all-start.1 = ((bf16[32,8,1792]{2,1,0:T(8,128)(2,1)}), bf16[32,8,1792]{2,1,0:T(8,128)(2,1)}, u32[]{:S(2)}, u32[]{:S(2)}) async-start(bf16[32,8,1792]{2,1,0:T(8,128)(2,1)} %bitcast.40), calls=%async_computation.1 | async-start | bytes 1835008 | tf_op jit(solution)/shard_map/all_to_all | solution.py:315
  36.0 6.3 %collective-permute-start.1 = (bf16[672,768]{1,0:T(8,128)(2,1)S(1)}, bf16[672,768]{1,0:T(8,128)(2,1)S(1)}, u32[]{:S(2)}, u32[]{:S(2)}) collective-permute-start(bf16[672,768]{1,0:T(8,128)(2,1)S(1)} %bitcast.33), channel_id=1, source_target_pairs={{0,128},{128,0},{1,129},{129,1},{2,130},{130,2},{3,131},{131,3},{4... | collective-permute-start | bytes 3096584 | tf_op jit(solution)/shard_map/ppermute | solution.py:309
  38.0 5.3 %collective-permute-start.2 = (bf16[672,768]{1,0:T(8,128)(2,1)S(1)}, bf16[672,768]{1,0:T(8,128)(2,1)}, u32[]{:S(2)}, u32[]{:S(2)}) collective-permute-start(bf16[672,768]{1,0:T(8,128)(2,1)S(1)} %bitcast.36), channel_id=1, source_target_pairs={{0,128},{128,0},{1,129},{129,1},{2,130},{130,2},{3,131},{131,3},{4... | collective-permute-start | bytes 3096584 | tf_op jit(solution)/shard_map/ppermute | solution.py:310
  40.4 53.4 %collective-permute-start = (bf16[672,768]{1,0:T(8,128)(2,1)}, bf16[672,768]{1,0:T(8,128)(2,1)}, u32[]{:S(2)}, u32[]{:S(2)}) collective-permute-start(bf16[672,768]{1,0:T(8,128)(2,1)} %bitcast.2.refs_0_), channel_id=1, source_target_pairs={{0,128},{128,0},{1,129},{129,1},{2,130},{130,2},{3,131},{131,3},{4... | collective-permute-start | bytes 3096584 | tf_op jit(solution)/shard_map/ppermute | solution.py:311
  42.3 1.0 copy-start.3
  64.3 39.9 %collective-permute-start.4 = (bf16[2,672,256]{2,1,0:T(8,128)(2,1)}, bf16[2,672,256]{2,1,0:T(8,128)(2,1)S(1)}, u32[]{:S(2)}, u32[]{:S(2)}) collective-permute-start(bf16[2,672,256]{2,1,0:T(8,128)(2,1)} %get-tuple-element.11), channel_id=1, source_target_pairs={{0,256},{256,0},{1,257},{257,1},{2,258},{258,2},{3,259},{259,3},{4... | collective-permute-start | bytes 2064392 | tf_op jit(solution)/shard_map/ppermute | solution.py:319
  93.8 10.4 %copy-start.4 = (bf16[2,672,256]{2,1,0:T(8,128)(2,1)S(1)}, bf16[2,672,256]{2,1,0:T(8,128)(2,1)}, u32[]{:S(2)}) copy-start(bf16[2,672,256]{2,1,0:T(8,128)(2,1)} %get-tuple-element.11) | copy-start | bytes 2064388
  97.6 15.8 %collective-permute-start.3 = (bf16[1,672,256]{2,1,0:T(8,128)(2,1)}, bf16[1,672,256]{2,1,0:T(8,128)(2,1)S(1)}, u32[]{:S(2)}, u32[]{:S(2)}) collective-permute-start(bf16[1,672,256]{2,1,0:T(8,128)(2,1)} %get-tuple-element.10.kept), channel_id=1, source_target_pairs={{0,256},{256,0},{1,257},{257,1},{2,258},{258,2},{3,259},{259,3},{4... | collective-permute-start | bytes 1032200 | tf_op jit(solution)/shard_map/ppermute | solution.py:322
  106.0 7.4 %copy-start.2 = (bf16[1,672,256]{2,1,0:T(8,128)(2,1)S(1)}, bf16[1,672,256]{2,1,0:T(8,128)(2,1)}, u32[]{:S(2)}) copy-start(bf16[1,672,256]{2,1,0:T(8,128)(2,1)} %get-tuple-element.10.kept) | copy-start | bytes 1032196
  115.7 25.6 %all-to-all-start.2 = ((bf16[32,8,1536]{2,1,0:T(8,128)(2,1)}), bf16[32,8,1536]{2,1,0:T(8,128)(2,1)S(1)}, u32[]{:S(2)}, u32[]{:S(2)}) async-start(bf16[32,8,1536]{2,1,0:T(8,128)(2,1)} %bitcast.41), calls=%async_computation.2 | async-start | bytes 1572864 | tf_op jit(solution)/shard_map/all_to_all | solution.py:340
  126.0 20.7 %collective-permute-start.5 = (bf16[1440,256]{1,0:T(8,128)(2,1)S(1)}, bf16[1440,256]{1,0:T(8,128)(2,1)}, u32[]{:S(2)}, u32[]{:S(2)}) collective-permute-start(bf16[1440,256]{1,0:T(8,128)(2,1)S(1)} %pad_maximum_fusion), channel_id=1, source_target_pairs={{0,128},{128,0},{1,129},{129,1},{2,130},{130,2},{3,131},{131,3},{4... | collective-permute-start | bytes 2211848 | tf_op jit(solution)/shard_map/ppermute | solution.py:329
  142.8 13.1 %all-to-all-start.3 = ((bf16[8,24,384]{2,1,0:T(8,128)(2,1)}), bf16[8,24,384]{2,1,0:T(8,128)(2,1)S(1)}, u32[]{:S(2)}, u32[]{:S(2)}) async-start(bf16[8,24,384]{2,1,0:T(8,128)(2,1)} %shard_map.92), calls=%async_computation.3 | async-start | bytes 294912 | tf_op jit(solution)/shard_map/all_to_all | solution.py:344
